TPU v7x, 32 devices: a whole 2x2x4 slice. The times are simulated.
32 devices in a mesh: seq: 16 (over z, y, core), head: 2 (over x).
Axes of the slice: x: 2, y: 2, z: 4, core: 2. Of those that a mesh axis runs over, the one named last changes fastest.
Arguments:
- queries: bfloat16 [2, 4096, 2048], P(None, 'seq', 'head'), may hold values from -8 to 8
- key_states: bfloat16 [2, 4096, 2048], P(None, 'seq', 'head'), may hold values from -8 to 8
- value_states: bfloat16 [2, 4096, 2048], P(None, 'seq', 'head'), may hold values from -6 to 6
- output_grad: bfloat16 [2, 4096, 2048], P(None, 'seq', 'head'), may hold values from -6 to 6
- out_proj: bfloat16 [2048, 2048], P('head'), may hold values from -0.125 to 0.125
Outputs:
- layer_out: bfloat16 [2, 4096, 2048], P(None, 'seq', 'head')
- query_grad: bfloat16 [2, 4096, 2048], P(None, 'seq', 'head')
- key_grad: bfloat16 [2, 4096, 2048], P(None, 'seq', 'head')
- value_grad: bfloat16 [2, 4096, 2048], P(None, 'seq', 'head')
All inputs are finite; a program needn't handle non-finite values.
Results may differ from a plain program's by a relative error of at most 0.012.
The roundings to bfloat16 on the way count: a program that leaves them out, or rounds other values in their place, can miss the bound.
Values may be sent and summed in bfloat16 or wider, within the bound.
No kernel may reach another device: no remote copies, remote signals or barrier semaphores. Data moves between devices by JAX's collectives and lax.ppermute only.
A program may use at most 192 MiB of HBM per device.

v0:
```python
from functools import partial

import jax
import jax.numpy as jnp
from jax import lax
from jax.sharding import PartitionSpec as P

HEAD_DIM = 128


def passed_along(shard, axis, by):
    length = lax.axis_size(axis)
    pairs = [(i, i + by) for i in range(length) if 0 <= i + by < length]
    return lax.ppermute(shard, axis, pairs)


def head_major(source):
    batch_rows, token_rows, features = source.shape
    return jnp.transpose(
        source.reshape(batch_rows, token_rows, features // HEAD_DIM, HEAD_DIM), (2, 0, 1, 3)
    )


def row_major(source):
    head_count, batch_rows, token_rows, features = source.shape
    return jnp.transpose(source, (1, 2, 0, 3)).reshape(
        batch_rows, token_rows, head_count * features
    )


def head_pass(pieces, key_mask, score_scale, whole):
    query_row_block, key_row_block, value_row_block, gradient_row_block = pieces
    own_rows = query_row_block.shape[1]
    scores = (
        jnp.einsum(
            "xei,xgi->xeg", query_row_block, key_row_block, preferred_element_type=jnp.float32
        )
        * score_scale
    )
    scores = jnp.where(key_mask, scores, -jnp.inf)
    maxima = jnp.max(scores, axis=2, keepdims=True)
    log_norm = maxima + jnp.log(jnp.sum(jnp.exp(scores - maxima), axis=2, keepdims=True))
    weights = jnp.exp(scores - log_norm)
    lower_weight_block = weights.astype(jnp.bfloat16)
    attn_block = jnp.einsum(
        "ifj,ijx->ifx", lower_weight_block, value_row_block, preferred_element_type=jnp.float32
    ).astype(jnp.bfloat16)
    row_dsum = jnp.sum(
        gradient_row_block.astype(jnp.float32) * attn_block.astype(jnp.float32),
        axis=2,
        keepdims=True,
    )
    grad_weights = jnp.einsum(
        "xei,xgi->xeg", gradient_row_block, value_row_block, preferred_element_type=jnp.float32
    )
    score_gradients = (weights * (grad_weights - row_dsum)).astype(jnp.bfloat16)
    dquery = (
        jnp.einsum(
            "ifj,ijx->ifx", score_gradients, key_row_block, preferred_element_type=jnp.float32
        )
        * score_scale
    ).astype(jnp.bfloat16)
    key_term = (
        jnp.einsum(
            "uwp,uwf->upf", score_gradients, query_row_block, preferred_element_type=jnp.float32
        )
        * score_scale
    )
    value_term = jnp.einsum(
        "uwp,uwf->upf", lower_weight_block, gradient_row_block, preferred_element_type=jnp.float32
    )
    return (
        attn_block,
        dquery,
        key_term[:, :own_rows],
        value_term[:, :own_rows],
        key_term[:, own_rows:].astype(jnp.bfloat16),
        value_term[:, own_rows:].astype(jnp.bfloat16),
    )


def body(queries, key_states, value_states, output_grad, out_proj):
    score_scale = HEAD_DIM ** (-0.5)
    levels = lax.axis_size("seq").bit_length() - 1
    seq_place = lax.axis_index("seq")
    own_rows = queries.shape[1]
    attn_grad = jnp.einsum(
        "brf,df->brd",
        lax.all_gather(output_grad, "head", axis=2, tiled=True),
        out_proj,
        preferred_element_type=jnp.float32,
    ).astype(jnp.bfloat16)
    causal = jnp.arange(own_rows)[:, None] >= jnp.arange(own_rows)[None, :]
    partner_flags = [seq_place // 2**bit_index % 2 == 1 for bit_index in range(levels)]
    key_mask = jnp.concatenate(
        [causal]
        + [jnp.broadcast_to(flag_value, (own_rows, own_rows)) for flag_value in partner_flags],
        axis=1,
    )
    key_parts = [key_states]
    value_parts = [value_states]
    for bit_index in range(levels):
        far_key, far_value = passed_along((key_states, value_states), "seq", 2**bit_index)
        key_parts.append(far_key)
        value_parts.append(far_value)
    pieces = (
        head_major(queries),
        head_major(jnp.concatenate(key_parts, axis=1)),
        head_major(jnp.concatenate(value_parts, axis=1)),
        head_major(attn_grad),
    )
    attn_heads, dquery_heads, own_key, own_value, far_keys, far_values = lax.map(
        partial(head_pass, key_mask=key_mask, score_scale=score_scale, whole=True), pieces
    )
    key_total = row_major(own_key)
    value_total = row_major(own_value)
    for bit_index in range(levels):
        low = bit_index * own_rows
        sent_key = row_major(far_keys[:, :, low : low + own_rows])
        sent_value = row_major(far_values[:, :, low : low + own_rows])
        back_key, back_value = passed_along((sent_key, sent_value), "seq", -(2**bit_index))
        key_total = key_total + back_key.astype(jnp.float32)
        value_total = value_total + back_value.astype(jnp.float32)
    attn_rows = row_major(attn_heads)
    query_grad = row_major(dquery_heads)
    partial_out = jnp.einsum("brd,df->brf", attn_rows, out_proj, preferred_element_type=jnp.float32)
    layer_out = lax.psum_scatter(partial_out, "head", scatter_dimension=2, tiled=True).astype(
        jnp.bfloat16
    )
    return (layer_out, query_grad, key_total.astype(jnp.bfloat16), value_total.astype(jnp.bfloat16))


def solution(mesh):
    in_specs = (
        P(None, "seq", "head"),
        P(None, "seq", "head"),
        P(None, "seq", "head"),
        P(None, "seq", "head"),
        P("head", None),
    )
    out_specs = (
        P(None, "seq", "head"),
        P(None, "seq", "head"),
        P(None, "seq", "head"),
        P(None, "seq", "head"),
    )
    return jax.shard_map(body, mesh=mesh, in_specs=in_specs, out_specs=out_specs, check_vma=False)
```

profile of v0, /device:TPU:13, one launch (start us, length us, event | category | flops | bytes accessed | tf_op | source)
XLA Modules:
  0.0 521.6 jit_solution(1665572796278092891)
XLA Ops:
  8.8 3.2 collective-permute-start.6
  12.0 3.1 collective-permute-start.5
  15.2 4.3 collective-permute-start.4
  26.1 8.7 %collective-permute-done.6 = bf16[2,256,1024]{1,2,0:T(8,128)(2,1)} collective-permute-done((bf16[2,256,1024]{1,2,0:T(8,128)(2,1)S(1)}, bf16[2,256,1024]{1,2,0:T(8,128)(2,1)}, u32[]{:S(2)}, u32[]{:S(2)}) %collective-permute-start.6) | collective-permute-done | bytes 1048608 | tf_op jit(solution)/shard_map/ppermute | solution.py:14
  34.8 3.2 collective-permute-start.1
  39.2 17.1 %collective-permute-done.5 = bf16[2,256,1024]{1,2,0:T(8,128)(2,1)} collective-permute-done((bf16[2,256,1024]{1,2,0:T(8,128)(2,1)S(1)}, bf16[2,256,1024]{1,2,0:T(8,128)(2,1)}, u32[]{:S(2)}, u32[]{:S(2)}) %collective-permute-start.5) | collective-permute-done | bytes 1048608 | tf_op jit(solution)/shard_map/ppermute | solution.py:14
  56.3 3.2 collective-permute-start.2
  59.5 41.3 %collective-permute-done.4 = bf16[2,256,1024]{1,2,0:T(8,128)(2,1)} collective-permute-done((bf16[2,256,1024]{1,2,0:T(8,128)(2,1)S(1)}, bf16[2,256,1024]{1,2,0:T(8,128)(2,1)}, u32[]{:S(2)}, u32[]{:S(2)}) %collective-permute-start.4) | collective-permute-done | bytes 1048608 | tf_op jit(solution)/shard_map/ppermute | solution.py:14
  106.1 17.7 %collective-permute-done.7 = bf16[2,256,1024]{1,2,0:T(8,128)(2,1)} collective-permute-done((bf16[2,256,1024]{1,2,0:T(8,128)(2,1)S(1)}, bf16[2,256,1024]{1,2,0:T(8,128)(2,1)}, u32[]{:S(2)}, u32[]{:S(2)}) %collective-permute-start.7) | collective-permute-done | bytes 1048608 | tf_op jit(solution)/shard_map/ppermute | solution.py:14
  125.0 32.4 %collective-permute-done = bf16[2,256,1024]{1,2,0:T(8,128)(2,1)} collective-permute-done((bf16[2,256,1024]{1,2,0:T(8,128)(2,1)S(1)}, bf16[2,256,1024]{1,2,0:T(8,128)(2,1)}, u32[]{:S(2)}, u32[]{:S(2)}) %collective-permute-start) | collective-permute-done | bytes 1048608 | tf_op jit(solution)/shard_map/ppermute | solution.py:14
  159.7 31.4 %collective-permute-done.1 = bf16[2,256,1024]{1,2,0:T(8,128)(2,1)S(1)} collective-permute-done((bf16[2,256,1024]{1,2,0:T(8,128)(2,1)S(1)}, bf16[2,256,1024]{1,2,0:T(8,128)(2,1)S(1)}, u32[]{:S(2)}, u32[]{:S(2)}) %collective-permute-start.1) | collective-permute-done | bytes 1048608 | tf_op jit(solution)/shard_map/ppermute | solution.py:14
  192.3 11.2 %collective-permute-done.2 = bf16[2,256,1024]{1,2,0:T(8,128)(2,1)S(1)} collective-permute-done((bf16[2,256,1024]{1,2,0:T(8,128)(2,1)S(1)}, bf16[2,256,1024]{1,2,0:T(8,128)(2,1)S(1)}, u32[]{:S(2)}, u32[]{:S(2)}) %collective-permute-start.2) | collective-permute-done | bytes 1048608 | tf_op jit(solution)/shard_map/ppermute | solution.py:14
  204.7 10.1 %collective-permute-done.3 = bf16[2,256,1024]{1,2,0:T(8,128)(2,1)S(1)} collective-permute-done((bf16[2,256,1024]{1,2,0:T(8,128)(2,1)S(1)}, bf16[2,256,1024]{1,2,0:T(8,128)(2,1)S(1)}, u32[]{:S(2)}, u32[]{:S(2)}) %collective-permute-start.3) | collective-permute-done | bytes 1048608 | tf_op jit(solution)/shard_map/ppermute | solution.py:14
  216.0 5.2 fusion.50
  222.1 99.9 %while.20 = (s32[]{:T(128)}, bf16[8,2,256,128]{2,3,0,1:T(8,128)(2,1)}, bf16[8,2,256,128]{3,2,1,0:T(8,128)(2,1)}, f32[8,2,256,128]{3,2,1,0:T(8,128)}, f32[8,2,256...) while((s32[]{:T(128)}, ...), condition=%wide.region_4.5_spmd, body=%wide.region_0.4_spmd.sunk | while | flops 1015938048 | bytes 26962072 | solution.py:112
  237.0 2.4 bitcast_dynamic-update-slice_fusion.2
  249.5 2.4 bitcast_dynamic-update-slice_fusion.2
  322.0 6.8 %fusion.38 = f32[2,256,2048]{2,1,0:T(8,128)} fusion(bf16[2,256,1024]{1,2,0:T(8,128)(2,1)} %bitcast.201, bf16[1024,2048]{1,0:T(8,128)(2,1)} %param.11), kind=kOutput, calls=%fused_computation.50 | convolution fusion | flops 2147483648 | bytes 9437184 | tf_op jit(solution)/shard_map/brd,df->brf/dot_general | solution.py:126
  328.9 4.0 slice_bitcast_fusion.5
  344.6 27.9 %collective-permute-done.8 = bf16[2,256,1024]{2,1,0:T(8,128)(2,1)S(1)} collective-permute-done((bf16[2,256,1024]{2,1,0:T(8,128)(2,1)S(1)}, bf16[2,256,1024]{2,1,0:T(8,128)(2,1)S(1)}, u32[]{:S(2)}, u32[]{:S(2)}) %collective-permute-start.8) | collective-permute-done | bytes 1048608 | tf_op jit(solution)/shard_map/ppermute | solution.py:14
  375.7 23.6 %collective-permute-done.10 = bf16[2,256,1024]{2,1,0:T(8,128)(2,1)S(1)} collective-permute-done((bf16[2,256,1024]{2,1,0:T(8,128)(2,1)S(1)}, bf16[2,256,1024]{2,1,0:T(8,128)(2,1)S(1)}, u32[]{:S(2)}, u32[]{:S(2)}) %collective-permute-start.10) | collective-permute-done | bytes 1048608 | tf_op jit(solution)/shard_map/ppermute | solution.py:14
  404.3 28.6 %collective-permute-done.14 = bf16[2,256,1024]{2,1,0:T(8,128)(2,1)S(1)} collective-permute-done((bf16[2,256,1024]{2,1,0:T(8,128)(2,1)S(1)}, bf16[2,256,1024]{2,1,0:T(8,128)(2,1)S(1)}, u32[]{:S(2)}, u32[]{:S(2)}) %collective-permute-start.14) | collective-permute-done | bytes 1048608 | tf_op jit(solution)/shard_map/ppermute | solution.py:14
  432.9 77.2 %collective-permute-done.12 = bf16[2,256,1024]{2,1,0:T(8,128)(2,1)S(1)} collective-permute-done((bf16[2,256,1024]{2,1,0:T(8,128)(2,1)S(1)}, bf16[2,256,1024]{2,1,0:T(8,128)(2,1)S(1)}, u32[]{:S(2)}, u32[]{:S(2)}) %collective-permute-start.12) | collective-permute-done | bytes 1048608 | tf_op jit(solution)/shard_map/ppermute | solution.py:14
  512.1 2.7 convert_element_type.57
  (154 shorter events, 139.1 us)
Async XLA Ops:
  7.2 14.6 %copy-start.3 = (bf16[2,256,1024]{2,1,0:T(8,128)(2,1)S(1)}, bf16[2,256,1024]{2,1,0:T(8,128)(2,1)}, u32[]{:S(2)}) copy-start(bf16[2,256,1024]{2,1,0:T(8,128)(2,1)} %param.8) | copy-start | bytes 3145732
  7.2 208.8 %all-gather.2.cloned.1.call-start = ((), (), s32[]{:S(2)}) async-start(), calls=%async_computation.1 | async-start | bytes 3145728 | tf_op jit(solution)/shard_map/all_gather | solution.py:89
  8.8 26.0 %collective-permute-start.6 = (bf16[2,256,1024]{1,2,0:T(8,128)(2,1)S(1)}, bf16[2,256,1024]{1,2,0:T(8,128)(2,1)}, u32[]{:S(2)}, u32[]{:S(2)}) collective-permute-start(bf16[2,256,1024]{1,2,0:T(8,128)(2,1)S(1)} %copy.42), channel_id=1, source_target_pairs={{0,8},{2,10},{4,12},{6,14},{8,16},{10,18},{12,20},{14,22},{16,24},... | collective-permute-start | bytes 3145736 | tf_op jit(solution)/shard_map/ppermute | solution.py:14
  12.0 44.3 %collective-permute-start.5 = (bf16[2,256,1024]{1,2,0:T(8,128)(2,1)S(1)}, bf16[2,256,1024]{1,2,0:T(8,128)(2,1)}, u32[]{:S(2)}, u32[]{:S(2)}) collective-permute-start(bf16[2,256,1024]{1,2,0:T(8,128)(2,1)S(1)} %copy.42), channel_id=1, source_target_pairs={{0,4},{2,6},{4,8},{6,10},{8,12},{10,14},{12,16},{14,18},{16,20},{1... | collective-permute-start | bytes 3145736 | tf_op jit(solution)/shard_map/ppermute | solution.py:14
  15.2 85.6 %collective-permute-start.4 = (bf16[2,256,1024]{1,2,0:T(8,128)(2,1)S(1)}, bf16[2,256,1024]{1,2,0:T(8,128)(2,1)}, u32[]{:S(2)}, u32[]{:S(2)}) collective-permute-start(bf16[2,256,1024]{1,2,0:T(8,128)(2,1)S(1)} %copy.42), channel_id=1, source_target_pairs={{0,2},{2,4},{4,6},{6,8},{8,10},{10,12},{12,14},{14,16},{16,18},{18... | collective-permute-start | bytes 3145736 | tf_op jit(solution)/shard_map/ppermute | solution.py:14
  19.5 492.6 %reduce-scatter.2.cloned.1.call-start = ((), (), s32[]{:S(2)}) async-start(), calls=%async_computation.2 | async-start | bytes 6291456 | tf_op jit(solution)/shard_map/reduce_scatter | solution.py:127
  19.5 104.2 %collective-permute-start.7 = (bf16[2,256,1024]{1,2,0:T(8,128)(2,1)S(1)}, bf16[2,256,1024]{1,2,0:T(8,128)(2,1)}, u32[]{:S(2)}, u32[]{:S(2)}) collective-permute-start(bf16[2,256,1024]{1,2,0:T(8,128)(2,1)S(1)} %copy.42), channel_id=1, source_target_pairs={{0,16},{2,18},{4,20},{6,22},{8,24},{10,26},{12,28},{14,30},{1,17},... | collective-permute-start | bytes 3145736 | tf_op jit(solution)/shard_map/ppermute | solution.py:14
  22.3 135.1 %collective-permute-start = (bf16[2,256,1024]{1,2,0:T(8,128)(2,1)S(1)}, bf16[2,256,1024]{1,2,0:T(8,128)(2,1)}, u32[]{:S(2)}, u32[]{:S(2)}) collective-permute-start(bf16[2,256,1024]{1,2,0:T(8,128)(2,1)S(1)} %copy.37), channel_id=1, source_target_pairs={{0,2},{2,4},{4,6},{6,8},{8,10},{10,12},{12,14},{14,16},{16,18},{18... | collective-permute-start | bytes 3145736 | tf_op jit(solution)/shard_map/ppermute | solution.py:14
  34.8 156.3 %collective-permute-start.1 = (bf16[2,256,1024]{1,2,0:T(8,128)(2,1)S(1)}, bf16[2,256,1024]{1,2,0:T(8,128)(2,1)S(1)}, u32[]{:S(2)}, u32[]{:S(2)}) collective-permute-start(bf16[2,256,1024]{1,2,0:T(8,128)(2,1)S(1)} %copy.37), channel_id=1, source_target_pairs={{0,4},{2,6},{4,8},{6,10},{8,12},{10,14},{12,16},{14,18},{16,20},{1... | collective-permute-start | bytes 3145736 | tf_op jit(solution)/shard_map/ppermute | solution.py:14
  56.3 147.3 %collective-permute-start.2 = (bf16[2,256,1024]{1,2,0:T(8,128)(2,1)S(1)}, bf16[2,256,1024]{1,2,0:T(8,128)(2,1)S(1)}, u32[]{:S(2)}, u32[]{:S(2)}) collective-permute-start(bf16[2,256,1024]{1,2,0:T(8,128)(2,1)S(1)} %copy.37), channel_id=1, source_target_pairs={{0,8},{2,10},{4,12},{6,14},{8,16},{10,18},{12,20},{14,22},{16,24},... | collective-permute-start | bytes 3145736 | tf_op jit(solution)/shard_map/ppermute | solution.py:14
  100.8 114.0 %collective-permute-start.3 = (bf16[2,256,1024]{1,2,0:T(8,128)(2,1)S(1)}, bf16[2,256,1024]{1,2,0:T(8,128)(2,1)S(1)}, u32[]{:S(2)}, u32[]{:S(2)}) collective-permute-start(bf16[2,256,1024]{1,2,0:T(8,128)(2,1)S(1)} %copy.37), channel_id=1, source_target_pairs={{0,16},{2,18},{4,20},{6,22},{8,24},{10,26},{12,28},{14,30},{1,17},... | collective-permute-start | bytes 3145736 | tf_op jit(solution)/shard_map/ppermute | solution.py:14
  125.0 79.6 %copy-start = (bf16[2,1280,1024]{1,2,0:T(8,128)(2,1)}, bf16[2,1280,1024]{1,2,0:T(8,128)(2,1)S(1)}, u32[]{:S(2)}) copy-start(bf16[2,1280,1024]{1,2,0:T(8,128)(2,1)S(1)} %constant_dynamic-update-slice_fusion.5) | copy-start | bytes 15728644
  333.5 39.0 %collective-permute-start.8 = (bf16[2,256,1024]{2,1,0:T(8,128)(2,1)S(1)}, bf16[2,256,1024]{2,1,0:T(8,128)(2,1)S(1)}, u32[]{:S(2)}, u32[]{:S(2)}) collective-permute-start(bf16[2,256,1024]{2,1,0:T(8,128)(2,1)S(1)} %bitcast.209), channel_id=1, source_target_pairs={{2,0},{4,2},{6,4},{8,6},{10,8},{12,10},{14,12},{16,14},{18,16},{20... | collective-permute-start | bytes 3145736 | tf_op jit(solution)/shard_map/ppermute | solution.py:14
  335.4 39.0 %collective-permute-start.11 = (bf16[2,256,1024]{2,1,0:T(8,128)(2,1)S(1)}, bf16[2,256,1024]{2,1,0:T(8,128)(2,1)S(1)}, u32[]{:S(2)}, u32[]{:S(2)}) collective-permute-start(bf16[2,256,1024]{2,1,0:T(8,128)(2,1)S(1)} %bitcast.205), channel_id=1, source_target_pairs={{16,0},{18,2},{20,4},{22,6},{24,8},{26,10},{28,12},{30,14},{17,1},... | collective-permute-start | bytes 3145736 | tf_op jit(solution)/shard_map/ppermute | solution.py:14
  337.0 62.2 %collective-permute-start.10 = (bf16[2,256,1024]{2,1,0:T(8,128)(2,1)S(1)}, bf16[2,256,1024]{2,1,0:T(8,128)(2,1)S(1)}, u32[]{:S(2)}, u32[]{:S(2)}) collective-permute-start(bf16[2,256,1024]{2,1,0:T(8,128)(2,1)S(1)} %bitcast.208), channel_id=1, source_target_pairs={{8,0},{10,2},{12,4},{14,6},{16,8},{18,10},{20,12},{22,14},{24,16},... | collective-permute-start | bytes 3145736 | tf_op jit(solution)/shard_map/ppermute | solution.py:14
  339.2 63.1 %collective-permute-start.9 = (bf16[2,256,1024]{2,1,0:T(8,128)(2,1)S(1)}, bf16[2,256,1024]{2,1,0:T(8,128)(2,1)S(1)}, u32[]{:S(2)}, u32[]{:S(2)}) collective-permute-start(bf16[2,256,1024]{2,1,0:T(8,128)(2,1)S(1)} %bitcast.206), channel_id=1, source_target_pairs={{4,0},{6,2},{8,4},{10,6},{12,8},{14,10},{16,12},{18,14},{20,16},{2... | collective-permute-start | bytes 3145736 | tf_op jit(solution)/shard_map/ppermute | solution.py:14
  341.9 59.2 %copy-start.4 = (bf16[8,2,256,128]{3,2,1,0:T(8,128)(2,1)S(1)}, bf16[8,2,256,128]{3,2,1,0:T(8,128)(2,1)}, u32[]{:S(2)}) copy-start(bf16[8,2,256,128]{3,2,1,0:T(8,128)(2,1)} %get-tuple-element.72) | copy-start | bytes 3145732
  342.2 60.1 %copy-start.2 = (f32[8,2,256,128]{3,2,1,0:T(8,128)S(1)}, f32[8,2,256,128]{3,2,1,0:T(8,128)}, u32[]{:S(2)}) copy-start(f32[8,2,256,128]{3,2,1,0:T(8,128)} %get-tuple-element.73) | copy-start | bytes 6291460
  342.5 61.8 %collective-permute-start.13 = (bf16[2,256,1024]{2,1,0:T(8,128)(2,1)S(1)}, bf16[2,256,1024]{2,1,0:T(8,128)(2,1)S(1)}, u32[]{:S(2)}, u32[]{:S(2)}) collective-permute-start(bf16[2,256,1024]{2,1,0:T(8,128)(2,1)S(1)} %bitcast.207), channel_id=1, source_target_pairs={{4,0},{6,2},{8,4},{10,6},{12,8},{14,10},{16,12},{18,14},{20,16},{2... | collective-permute-start | bytes 3145736 | tf_op jit(solution)/shard_map/ppermute | solution.py:14
  372.4 60.5 %collective-permute-start.14 = (bf16[2,256,1024]{2,1,0:T(8,128)(2,1)S(1)}, bf16[2,256,1024]{2,1,0:T(8,128)(2,1)S(1)}, u32[]{:S(2)}, u32[]{:S(2)}) collective-permute-start(bf16[2,256,1024]{2,1,0:T(8,128)(2,1)S(1)} %bitcast.204), channel_id=1, source_target_pairs={{8,0},{10,2},{12,4},{14,6},{16,8},{18,10},{20,12},{22,14},{24,16},... | collective-permute-start | bytes 3145736 | tf_op jit(solution)/shard_map/ppermute | solution.py:14
  374.4 58.6 %collective-permute-start.15 = (bf16[2,256,1024]{2,1,0:T(8,128)(2,1)S(1)}, bf16[2,256,1024]{2,1,0:T(8,128)(2,1)S(1)}, u32[]{:S(2)}, u32[]{:S(2)}) collective-permute-start(bf16[2,256,1024]{2,1,0:T(8,128)(2,1)S(1)} %bitcast.203), channel_id=1, source_target_pairs={{16,0},{18,2},{20,4},{22,6},{24,8},{26,10},{28,12},{30,14},{17,1},... | collective-permute-start | bytes 3145736 | tf_op jit(solution)/shard_map/ppermute | solution.py:14
  399.2 110.9 %collective-permute-start.12 = (bf16[2,256,1024]{2,1,0:T(8,128)(2,1)S(1)}, bf16[2,256,1024]{2,1,0:T(8,128)(2,1)S(1)}, u32[]{:S(2)}, u32[]{:S(2)}) collective-permute-start(bf16[2,256,1024]{2,1,0:T(8,128)(2,1)S(1)} %bitcast.202), channel_id=1, source_target_pairs={{2,0},{4,2},{6,4},{8,6},{10,8},{12,10},{14,12},{16,14},{18,16},{20... | collective-permute-start | bytes 3145736 | tf_op jit(solution)/shard_map/ppermute | solution.py:14
  402.3 107.8 %copy-start.1 = (f32[8,2,256,128]{3,2,1,0:T(8,128)S(1)}, f32[8,2,256,128]{3,2,1,0:T(8,128)}, u32[]{:S(2)}) copy-start(f32[8,2,256,128]{3,2,1,0:T(8,128)} %get-tuple-element.75) | copy-start | bytes 6291460
Sparse Core Ops, SparseCore 0:
  19.6 31.6 all-gather.1
  329.0 55.3 reduce-scatter.1
where the time goes:
time: 524 us; the launch traced here: 522 us
  waiting for transfers between devices  327 us (62%)
  matrix products  90.6 us (17%)
  local copies, waits for them, and re-layouts  40.4 us (8%)
  starting transfers between devices  37.1 us (7%)
  between operations  14.6 us (3%)
  other arithmetic  11.6 us (2%)
    ppermute x16, waiting for transfers between devices, passed_along(): return lax.ppermute(shard, axis, pairs)  327 us
    ppermute x16, starting transfers between devices, passed_along(): return lax.ppermute(shard, axis, pairs)  37 us
    dot_general x8, matrix products, head_pass(): jnp.einsum('ifj,ijx->ifx', lower_weight_block, value_row_block, preferred...  19.5 us
    dot_general x8, matrix products, head_pass(): jnp.einsum('ifj,ijx->ifx', score_gradients, key_row_block, preferred_elem...  18 us
    unnamed x26, local copies, waits for them, and re-layouts  17.6 us
    dynamic_update_slice x16, local copies, waits for them, and re-layouts, body(): lax.map(partial(head_pass, key_mask=key_mask, score_scale=score_scale, wh...  16.2 us
    dot_general x8, matrix products, head_pass(): jnp.einsum('xei,xgi->xeg', query_row_block, key_row_block, preferred_elem...  14.9 us
    dot_general x8, matrix products, head_pass(): jnp.einsum('xei,xgi->xeg', gradient_row_block, value_row_block, preferred...  14.7 us
  transfers between devices with their start and end apart: 18, of which 12 were waited for; matrix products, arithmetic and copies ran while one was open for 5% of the time, Pallas kernels for 0%

commit v1 on v0

v1 whole, which is shorter than its diff:
```python
from functools import partial

import jax
import jax.numpy as jnp
from jax import lax
from jax.experimental import pallas as pl
from jax.experimental.pallas import tpu as pltpu
from jax.sharding import PartitionSpec as P

HEAD_DIM = 128
COARSE_LEVELS = 2
LOG2_E = 1.4426950408889634
FAR_OFF = 1e30
VMEM_LIMIT = 24 * 1024 * 1024


def dot_t(a, b):
    return lax.dot_general(a, b, (((1,), (1,)), ((), ())), preferred_element_type=jnp.float32)


def dot_n(a, b):
    return lax.dot_general(a, b, (((1,), (0,)), ((), ())), preferred_element_type=jnp.float32)


def dot_l(a, b):
    return lax.dot_general(a, b, (((0,), (0,)), ((), ())), preferred_element_type=jnp.float32)


def unit_kernel(levels, fine, coarse, has_next, n_alias, scalars, *refs):
    refs = list(refs)
    q_ref, k_ref, v_ref, grad_own, grad_other, proj_own, proj_other = refs[:7]
    refs = refs[7:]
    far_refs = refs[:levels]
    refs = refs[levels:]
    if has_next:
        next_k, next_v = refs[:2]
        refs = refs[2:]
    refs = refs[n_alias:]
    attn_ref, dq_ref, own_ref = refs[:3]
    refs = refs[3:]
    coarse_refs = refs[: len(coarse)]
    refs = refs[len(coarse) :]
    fine_refs = refs[: len(fine)]
    refs = refs[len(fine) :]
    weight_scr, low_scr = refs

    scale = HEAD_DIM ** (-0.5)
    rows = q_ref.shape[1]
    queries = q_ref[0]
    grad_t = (
        dot_t(proj_own[...], grad_own[0]) + dot_t(proj_other[...], grad_other[0])
    ).astype(jnp.bfloat16)

    def keys_of(index):
        return k_ref[0] if index == 0 else far_refs[index - 1][0]

    def values_of(index):
        return v_ref[0] if index == 0 else far_refs[index - 1][1]

    def span(index):
        return pl.ds(index * rows, rows)

    shift = [jnp.float32(0.0)]
    for level in range(levels):
        shift.append(jnp.where(scalars[2 + level] == 1, jnp.float32(0.0), jnp.float32(FAR_OFF)))

    maxima = None
    for index in range(levels + 1):
        scores = dot_t(keys_of(index), queries) * jnp.float32(scale * LOG2_E)
        if index == 0:
            key_at = lax.broadcasted_iota(jnp.int32, scores.shape, 0)
            query_at = lax.broadcasted_iota(jnp.int32, scores.shape, 1)
            scores = jnp.where(key_at <= query_at, scores, -jnp.float32(FAR_OFF))
        weight_scr[span(index), :] = scores
        top = jnp.max(scores, axis=0, keepdims=True) - shift[index]
        maxima = top if maxima is None else jnp.maximum(maxima, top)
    total = None
    for index in range(levels + 1):
        powers = jnp.exp2(weight_scr[span(index), :] - (maxima + shift[index]))
        weight_scr[span(index), :] = powers
        part = jnp.sum(powers, axis=0, keepdims=True)
        total = part if total is None else total + part
    inverse = 1.0 / total
    attn_t = None
    for index in range(levels + 1):
        weights = weight_scr[span(index), :] * inverse
        weight_scr[span(index), :] = weights
        low = weights.astype(jnp.bfloat16)
        low_scr[span(index), :] = low
        part = dot_l(values_of(index), low)
        attn_t = part if attn_t is None else attn_t + part
    attn_t = attn_t.astype(jnp.bfloat16).astype(jnp.float32)
    attn_ref[...] = attn_t.T.astype(jnp.bfloat16)
    row_dsum = jnp.sum(grad_t.astype(jnp.float32) * attn_t, axis=0, keepdims=True)

    dq_t = None
    for index in range(levels + 1):
        low = low_scr[span(index), :]
        value_term = dot_t(low, grad_t)
        grad_weights = dot_n(values_of(index), grad_t)
        grad_scores = (weight_scr[span(index), :] * (grad_weights - row_dsum)).astype(jnp.bfloat16)
        key_term = dot_n(grad_scores, queries) * scale
        part = dot_l(keys_of(index), grad_scores)
        dq_t = part if dq_t is None else dq_t + part
        if index == 0:
            own_ref[0] = key_term
            own_ref[1] = value_term
        else:
            level = index - 1
            if level in coarse:
                target = coarse_refs[coarse.index(level)]
            else:
                target = fine_refs[fine.index(level)]
            target[0] = key_term.astype(jnp.bfloat16)
            target[1] = value_term.astype(jnp.bfloat16)
            if has_next and level in fine:

                @pl.when(scalars[2 + level] == 0)
                def _():
                    target[0] = next_k[0]
                    target[1] = next_v[0]

    dq_ref[0] = (dq_t * scale).T.astype(jnp.bfloat16)


def chunk_call(levels, fine, coarse, chunk, upcoming, far_at, down_at, down_units, scalars, arrays, far, carried):
    queries, keys, values, output_grad, other_grad, out_proj = arrays
    batch_at, head_at, count = chunk
    rows, width = queries.shape[1], queries.shape[2]
    has_next = upcoming is not None
    wide = out_proj.shape[1] // 2

    def of_unit(batch, head):
        return pl.BlockSpec((1, rows, HEAD_DIM), lambda i, s, b=batch, h=head: (b, 0, h + i))

    in_specs = [
        of_unit(batch_at, head_at),
        of_unit(batch_at, head_at),
        of_unit(batch_at, head_at),
        pl.BlockSpec((1, rows, wide), lambda i, s: (batch_at, 0, 0)),
        pl.BlockSpec((1, rows, wide), lambda i, s: (0, 0, 0)),
        pl.BlockSpec((HEAD_DIM, wide), lambda i, s: (head_at + i, s[0])),
        pl.BlockSpec((HEAD_DIM, wide), lambda i, s: (head_at + i, s[1])),
    ]
    operands = [queries, keys, values, output_grad, other_grad, out_proj, out_proj]
    for level in range(levels):
        in_specs.append(
            pl.BlockSpec((2, rows, HEAD_DIM), lambda i, s, h=far_at[level]: (0, 0, h + i))
        )
        operands.append(far[level])
    if has_next:
        in_specs += [of_unit(*upcoming[:2])] * 2
        operands += [keys, values]

    out_shapes = [
        jax.ShapeDtypeStruct((rows, width), jnp.bfloat16),
        jax.ShapeDtypeStruct(queries.shape, jnp.bfloat16),
        jax.ShapeDtypeStruct((2, rows, width), jnp.float32),
    ]
    out_specs = [
        pl.BlockSpec((rows, HEAD_DIM), lambda i, s: (0, head_at + i)),
        of_unit(batch_at, head_at),
        pl.BlockSpec((2, rows, HEAD_DIM), lambda i, s: (0, 0, head_at + i)),
    ]
    for place, level in enumerate(coarse):
        out_shapes.append(
            jax.ShapeDtypeStruct((2, rows, down_units[place] * HEAD_DIM), jnp.bfloat16)
        )
        out_specs.append(
            pl.BlockSpec((2, rows, HEAD_DIM), lambda i, s, h=down_at[place]: (0, 0, h + i))
        )
    for level in fine:
        out_shapes.append(jax.ShapeDtypeStruct((2, rows, count * HEAD_DIM), jnp.bfloat16))
        out_specs.append(pl.BlockSpec((2, rows, HEAD_DIM), lambda i, s: (0, 0, i)))

    aliases = {}
    for place, held in enumerate(carried):
        if held is not None:
            aliases[1 + len(operands)] = place
            in_specs.append(pl.BlockSpec(memory_space=pl.ANY))
            operands.append(held)
    seen = (levels + 1) * rows
    flops = count * 2 * (6 * seen * rows * HEAD_DIM + 2 * rows * wide * HEAD_DIM)
    return pl.pallas_call(
        partial(unit_kernel, levels, fine, coarse, has_next, len(aliases)),
        out_shape=out_shapes,
        grid_spec=pltpu.PrefetchScalarGridSpec(
            num_scalar_prefetch=1,
            grid=(count,),
            in_specs=in_specs,
            out_specs=out_specs,
            scratch_shapes=[
                pltpu.VMEM((seen, rows), jnp.float32),
                pltpu.VMEM((seen, rows), jnp.bfloat16),
            ],
        ),
        input_output_aliases=aliases,
        compiler_params=pltpu.CompilerParams(vmem_limit_bytes=VMEM_LIMIT),
        cost_estimate=pl.CostEstimate(
            flops=flops, bytes_accessed=count * 4 * 2**20, transcendentals=count * seen * rows
        ),
    )(scalars, *operands)


def project_kernel(scalars, attn_ref, proj_ref, send_ref, own_ref):
    step = pl.program_id(0)
    product = dot_n(attn_ref[...], proj_ref[...])

    @pl.when(step < 2)
    def _():
        send_ref[...] = product.astype(jnp.bfloat16)

    @pl.when(step >= 2)
    def _():
        own_ref[...] = product


def project(scalars, attn, out_proj):
    rows, depth = attn.shape
    wide = out_proj.shape[1] // 2
    block = wide // 2
    return pl.pallas_call(
        project_kernel,
        out_shape=[
            jax.ShapeDtypeStruct((rows, wide), jnp.bfloat16),
            jax.ShapeDtypeStruct((rows, wide), jnp.float32),
        ],
        grid_spec=pltpu.PrefetchScalarGridSpec(
            num_scalar_prefetch=1,
            grid=(4,),
            in_specs=[
                pl.BlockSpec((rows, depth), lambda i, s: (0, 0)),
                pl.BlockSpec(
                    (depth, block), lambda i, s: (0, jnp.where(i < 2, s[1], s[0]) * 2 + i % 2)
                ),
            ],
            out_specs=[
                pl.BlockSpec((rows, block), lambda i, s: (0, jnp.minimum(i, 1))),
                pl.BlockSpec((rows, block), lambda i, s: (0, jnp.maximum(i - 2, 0))),
            ],
        ),
        compiler_params=pltpu.CompilerParams(vmem_limit_bytes=VMEM_LIMIT),
        cost_estimate=pl.CostEstimate(
            flops=4 * rows * depth * wide, bytes_accessed=6 * 2**20, transcendentals=0
        ),
    )(scalars, attn, out_proj)


def finish_kernel(levels, masked, scalars, *refs):
    own_ref, far_refs = refs[0], refs[1 : 1 + levels]
    key_ref, value_ref = refs[-2:]
    for place, target in enumerate((key_ref, value_ref)):
        total = own_ref[place]
        for level in range(levels):
            term = far_refs[level][place].astype(jnp.float32)
            if masked[level]:
                term = jnp.where(scalars[2 + level] == 1, jnp.zeros_like(term), term)
            total = total + term
        target[0] = total.astype(jnp.bfloat16)


def finish(levels, masked, chunk, far_at, shape, scalars, own, far, carried):
    batch_at, head_at, count = chunk
    rows = shape[1]
    in_specs = [pl.BlockSpec((2, rows, HEAD_DIM), lambda i, s: (0, 0, head_at + i))]
    operands = [own]
    for level in range(levels):
        in_specs.append(
            pl.BlockSpec((2, rows, HEAD_DIM), lambda i, s, h=far_at[level]: (0, 0, h + i))
        )
        operands.append(far[level])
    aliases = {}
    for place, held in enumerate(carried):
        if held is not None:
            aliases[1 + len(operands)] = place
            in_specs.append(pl.BlockSpec(memory_space=pl.ANY))
            operands.append(held)
    out_spec = pl.BlockSpec((1, rows, HEAD_DIM), lambda i, s: (batch_at, 0, head_at + i))
    return pl.pallas_call(
        partial(finish_kernel, levels, masked),
        out_shape=[jax.ShapeDtypeStruct(shape, jnp.bfloat16)] * 2,
        grid_spec=pltpu.PrefetchScalarGridSpec(
            num_scalar_prefetch=1, grid=(count,), in_specs=in_specs, out_specs=[out_spec] * 2
        ),
        input_output_aliases=aliases,
        compiler_params=pltpu.CompilerParams(vmem_limit_bytes=VMEM_LIMIT),
        cost_estimate=pl.CostEstimate(
            flops=count * 2 * (levels + 1) * rows * HEAD_DIM,
            bytes_accessed=count * rows * HEAD_DIM * 4 * (levels + 3),
            transcendentals=0,
        ),
    )(scalars, *operands)


def groups_of(sizes, heads):
    out, at = [], 0
    for size in sizes:
        out.append((at // heads, at % heads, size))
        at += size
    return out


def holder(groups, chunk):
    for index, (batch, head, count) in enumerate(groups):
        if batch == chunk[0] and head <= chunk[1] < head + count:
            return index, chunk[1] - head
    raise ValueError("chunk")


def body(queries, key_states, value_states, output_grad, out_proj):
    batch, rows, width = queries.shape
    heads = width // HEAD_DIM
    seq_size = lax.axis_size("seq")
    levels = seq_size.bit_length() - 1
    coarse = list(range(min(COARSE_LEVELS, levels)))
    fine = list(range(len(coarse), levels))
    place = lax.axis_index("seq")
    half = lax.axis_index("head")
    scalars = jnp.stack(
        [half, 1 - half] + [place // 2**level % 2 for level in range(levels)]
    ).astype(jnp.int32)

    step = 2
    units = batch * heads
    chunks = groups_of([step] * (units // step), heads)
    count = len(chunks)
    split = [[heads] * batch, [step, heads - step] + [heads] * (batch - 1)]
    split_down = [[heads] * batch, [heads] * (batch - 1) + [heads - step, step]]
    ups = [groups_of(split[level], heads) for level in coarse]
    downs = [groups_of(split_down[level], heads) for level in coarse]

    lower = [[i for i in range(seq_size) if not (i >> level) & 1] for level in range(levels)]
    up_pairs = [[(i, i + 2**level) for i in lower[level]] for level in range(levels)]
    down_pairs = [[(i + 2**level, i) for i in lower[level]] for level in range(levels)]

    def packed(group):
        at, head, number = group
        low, high = head * HEAD_DIM, (head + number) * HEAD_DIM
        return jnp.stack([key_states[at, :, low:high], value_states[at, :, low:high]])

    def other_half(source):
        return lax.ppermute(source, "head", [(0, 1), (1, 0)])

    far_fine = {}
    for t in range(2):
        buffer = packed(chunks[t])
        for level in reversed(fine):
            far_fine[level, t] = lax.ppermute(buffer, "seq", up_pairs[level])
    other_grads = [other_half(output_grad[at : at + 1]) for at in range(batch)]
    far_coarse = {
        (level, index): lax.ppermute(packed(group), "seq", up_pairs[level])
        for level in reversed(coarse)
        for index, group in enumerate(ups[level])
    }

    attn = [None] * batch
    own = [None] * batch
    query_grad = None
    down_buffers = {}
    back_coarse = {}
    layer_parts = []
    grads = (None, None)

    def finished(c, grads):
        chunk = chunks[c]
        far, far_at, masked = [], [], []
        for level in range(levels):
            if level in coarse:
                index, at = holder(downs[level], chunk)
                far.append(back_coarse[level, index])
                masked.append(False)
            else:
                far.append(far_fine[level, c + 2])
                at = 0
                masked.append(c + 2 < count)
            far_at.append(at)
        return finish(
            levels, masked, chunk, far_at, queries.shape, scalars, own[chunk[0]], far, grads
        )

    for t, chunk in enumerate(chunks):
        at = chunk[0]
        upcoming = chunks[t + 2] if t + 2 < count else None
        far, far_at, down_at, down_units, down_index = [], [], [], [], []
        for level in range(levels):
            if level in coarse:
                index, offset = holder(ups[level], chunk)
                far.append(far_coarse[level, index])
                index, down_offset = holder(downs[level], chunk)
                down_index.append(index)
                down_at.append(down_offset)
                down_units.append(downs[level][index][2])
            else:
                far.append(far_fine[level, t])
                offset = 0
            far_at.append(offset)
        carried = [attn[at], query_grad, own[at]] + [
            down_buffers.get((level, down_index[level])) for level in coarse
        ]
        results = chunk_call(
            levels,
            fine,
            coarse,
            chunk,
            upcoming,
            far_at,
            down_at,
            down_units,
            scalars,
            (queries, key_states, value_states, output_grad, other_grads[at], out_proj),
            far,
            carried,
        )
        attn[at], query_grad, own[at] = results[:3]
        for level in coarse:
            down_buffers[level, down_index[level]] = results[3 + level]
            group = downs[level][down_index[level]]
            if group[0] == at and group[1] + group[2] == chunk[1] + chunk[2]:
                back_coarse[level, down_index[level]] = lax.ppermute(
                    results[3 + level], "seq", down_pairs[level]
                )
        for place_of, level in reversed(list(enumerate(fine))):
            pairs = down_pairs[level] + (up_pairs[level] if upcoming is not None else [])
            far_fine[level, t + 2] = lax.ppermute(results[3 + len(coarse) + place_of], "seq", pairs)
        if chunk[1] + chunk[2] == heads:
            send, kept = project(scalars, attn[at], out_proj)
            layer_parts.append(kept + other_half(send).astype(jnp.float32))
    for c in range(count):
        grads = finished(c, grads)
    layer_out = jnp.stack(layer_parts).astype(jnp.bfloat16)
    return layer_out, query_grad, grads[0], grads[1]


def solution(mesh):
    spec = P(None, "seq", "head")
    return jax.shard_map(
        body,
        mesh=mesh,
        in_specs=(spec, spec, spec, spec, P("head", None)),
        out_specs=(spec, spec, spec, spec),
        check_vma=False,
    )
```

time: 524 us -> 192 us (0.37)
  the two profiles are of different devices: /device:TPU:13 before, /device:TPU:0 now
where the time goes in v1:
time: 192 us
  Pallas kernels  83.3 us (43%)
  starting transfers between devices  63.7 us (33%)
  waiting for transfers between devices  26.5 us (14%)
  local copies, waits for them, and re-layouts  12.9 us (7%)
  other arithmetic  4.24 us (2%)
    pallas_call x8, Pallas kernels, chunk_call(): pl.pallas_call(partial(unit_kernel, levels, fine, coarse, has_next, len(a...  63.3 us
    ppermute x4, starting transfers between devices, body(): far_fine[level, t] = lax.ppermute(buffer, 'seq', up_pairs[level])  20.5 us
    ppermute x16, starting transfers between devices, body(): lax.ppermute(results[3 + len(coarse) + place_of], 'seq', pairs)  17 us
    ppermute x16, waiting for transfers between devices, body(): lax.ppermute(results[3 + len(coarse) + place_of], 'seq', pairs)  15.7 us
    ppermute x5, starting transfers between devices, body(): lax.ppermute(packed(group), 'seq', up_pairs[level])  14.6 us
    pallas_call x8, Pallas kernels, finish(): pl.pallas_call(partial(finish_kernel, levels, masked), out_shape=[jax.Sha...  13.9 us
    unnamed x32, local copies, waits for them, and re-layouts  10.1 us
    ppermute x5, waiting for transfers between devices, body(): lax.ppermute(results[3 + level], 'seq', down_pairs[level])  7.31 us
  transfers between devices with their start and end apart: 34, of which 11 were waited for; matrix products, arithmetic and copies ran while one was open for 3% of the time, Pallas kernels for 43%

profile of v1, /device:TPU:0, one launch (start us, length us, event | category | flops | bytes accessed | tf_op | source)
XLA Modules:
  0.0 191.6 jit_solution(14179846460061644051)
XLA Ops:
  2.5 2.7 %collective-permute-start.1 = (bf16[2,256,1024]{2,1,0:T(8,128)(2,1)S(1)}, bf16[2,256,1024]{2,1,0:T(8,128)(2,1)S(1)}, u32[]{:S(2)}, u32[]{:S(2)}) collective-permute-start(bf16[2,256,1024]{2,1,0:T(8,128)(2,1)S(1)} %pad_maximum_fusion), channel_id=1, source_target_pairs={{0,2},{4,6},{8,10},{12,14},{16,18},{20,22},{24,26},{28,30},{1,3},{... | collective-permute-start | bytes 3145736 | tf_op jit(solution)/shard_map/ppermute | solution.py:351
  5.3 4.3 %collective-permute-start.5 = (bf16[2,256,256]{2,1,0:T(8,128)(2,1)S(1)}, bf16[2,256,256]{2,1,0:T(8,128)(2,1)S(1)}, u32[]{:S(2)}, u32[]{:S(2)}) collective-permute-start(bf16[2,256,256]{2,1,0:T(8,128)(2,1)S(1)} %pad_maximum_fusion.5), channel_id=1, source_target_pairs={{0,4},{2,6},{8,12},{10,14},{16,20},{18,22},{24,28},{26,30},{1,5},{... | collective-permute-start | bytes 786440 | tf_op jit(solution)/shard_map/ppermute | solution.py:351
  15.2 3.5 %collective-permute-start.6 = (bf16[2,256,256]{2,1,0:T(8,128)(2,1)S(1)}, bf16[2,256,256]{2,1,0:T(8,128)(2,1)S(1)}, u32[]{:S(2)}, u32[]{:S(2)}) collective-permute-start(bf16[2,256,256]{2,1,0:T(8,128)(2,1)S(1)} %pad_maximum_fusion.5), channel_id=1, source_target_pairs={{0,8},{2,10},{4,12},{6,14},{16,24},{18,26},{20,28},{22,30},{1,9},{... | collective-permute-start | bytes 786440 | tf_op jit(solution)/shard_map/ppermute | solution.py:348
  18.7 4.5 %collective-permute-start.7 = (bf16[2,256,256]{2,1,0:T(8,128)(2,1)S(1)}, bf16[2,256,256]{2,1,0:T(8,128)(2,1)S(1)}, u32[]{:S(2)}, u32[]{:S(2)}) collective-permute-start(bf16[2,256,256]{2,1,0:T(8,128)(2,1)S(1)} %pad_maximum_fusion.5), channel_id=1, source_target_pairs={{0,16},{2,18},{4,20},{6,22},{8,24},{10,26},{12,28},{14,30},{1,17},... | collective-permute-start | bytes 786440 | tf_op jit(solution)/shard_map/ppermute | solution.py:348
  24.4 2.3 %collective-permute-start.14 = (bf16[2,256,1024]{2,1,0:T(8,128)(2,1)}, bf16[2,256,1024]{2,1,0:T(8,128)(2,1)}, u32[]{:S(2)}, u32[]{:S(2)}) collective-permute-start(bf16[2,256,1024]{2,1,0:T(8,128)(2,1)} %pad_maximum_fusion.1), channel_id=1, source_target_pairs={{0,2},{4,6},{8,10},{12,14},{16,18},{20,22},{24,26},{28,30},{1,3},{... | collective-permute-start | bytes 3145736 | tf_op jit(solution)/shard_map/ppermute | solution.py:351
  29.5 6.5 %collective-permute-start.3 = (bf16[2,256,256]{2,1,0:T(8,128)(2,1)}, bf16[2,256,256]{2,1,0:T(8,128)(2,1)}, u32[]{:S(2)}, u32[]{:S(2)}) collective-permute-start(bf16[2,256,256]{2,1,0:T(8,128)(2,1)} %pad_maximum_fusion.4), channel_id=1, source_target_pairs={{0,8},{2,10},{4,12},{6,14},{16,24},{18,26},{20,28},{22,30},{1,9},{... | collective-permute-start | bytes 786440 | tf_op jit(solution)/shard_map/ppermute | solution.py:348
  36.8 6.0 %collective-permute-start.4 = (bf16[2,256,256]{2,1,0:T(8,128)(2,1)}, bf16[2,256,256]{2,1,0:T(8,128)(2,1)}, u32[]{:S(2)}, u32[]{:S(2)}) collective-permute-start(bf16[2,256,256]{2,1,0:T(8,128)(2,1)} %pad_maximum_fusion.4), channel_id=1, source_target_pairs={{0,16},{2,18},{4,20},{6,22},{8,24},{10,26},{12,28},{14,30},{1,17},... | collective-permute-start | bytes 786440 | tf_op jit(solution)/shard_map/ppermute | solution.py:348
  43.8 3.1 %collective-permute-start.15 = (bf16[2,256,1024]{2,1,0:T(8,128)(2,1)}, bf16[2,256,1024]{2,1,0:T(8,128)(2,1)}, u32[]{:S(2)}, u32[]{:S(2)}) collective-permute-start(bf16[2,256,1024]{2,1,0:T(8,128)(2,1)} %pad_maximum_fusion.1), channel_id=1, source_target_pairs={{0,4},{2,6},{8,12},{10,14},{16,20},{18,22},{24,28},{26,30},{1,5},{... | collective-permute-start | bytes 3145736 | tf_op jit(solution)/shard_map/ppermute | solution.py:351
  54.6 7.5 %shard_map.84 = (bf16[256,1024]{1,0:T(8,128)(2,1)S(1)}, bf16[2,256,1024]{2,1,0:T(8,128)(2,1)}, f32[2,256,1024]{2,1,0:T(8,128)S(1)}, bf16[2,256,1024]{2,1,0:T(8,1...) custom-call(s32[6]{0:T(128)S(1)} %stack.56.scalars, ...), custom_call_target="tpu_custom_call" | custom-call | flops 1275068416 | bytes 8388608 | tf_op jit(solution)/shard_map/pallas_call | solution.py:184
  63.7 8.1 %shard_map.85 = (bf16[256,1024]{1,0:T(8,128)(2,1)S(1)}, bf16[2,256,1024]{2,1,0:T(8,128)(2,1)}, f32[2,256,1024]{2,1,0:T(8,128)S(1)}, bf16[2,256,1024]{2,1,0:T(8,1...) custom-call(s32[6]{0:T(128)S(1)} %stack.56.scalars, ...), custom_call_target="tpu_custom_call", output_to_operand_aliasing={{0}: (14, {}), {1}: (15, {}), {2}: (16, {}), {3}: (17, {}),... | custom-call | flops 1275068416 | bytes 8388608 | tf_op jit(solution)/shard_map/pallas_call | solution.py:184
  76.7 8.0 %shard_map.86 = (bf16[256,1024]{1,0:T(8,128)(2,1)S(1)}, bf16[2,256,1024]{2,1,0:T(8,128)(2,1)}, f32[2,256,1024]{2,1,0:T(8,128)S(1)}, bf16[2,256,1024]{2,1,0:T(8,1...) custom-call(s32[6]{0:T(128)S(1)} %stack.56.scalars, ...), custom_call_target="tpu_custom_call", output_to_operand_aliasing={{0}: (14, {}), {1}: (15, {}), {2}: (16, {}), {3}: (17, {}),... | custom-call | flops 1275068416 | bytes 8388608 | tf_op jit(solution)/shard_map/pallas_call | solution.py:184
  87.1 8.4 %shard_map.87 = (bf16[256,1024]{1,0:T(8,128)(2,1)S(1)}, bf16[2,256,1024]{2,1,0:T(8,128)(2,1)}, f32[2,256,1024]{2,1,0:T(8,128)S(1)}, bf16[2,256,1024]{2,1,0:T(8,1...) custom-call(s32[6]{0:T(128)S(1)} %stack.56.scalars, ...), custom_call_target="tpu_custom_call", output_to_operand_aliasing={{0}: (14, {}), {1}: (15, {}), {2}: (16, {}), {3}: (17, {}),... | custom-call | flops 1275068416 | bytes 8388608 | tf_op jit(solution)/shard_map/pallas_call | solution.py:184
  98.8 2.5 %collective-permute-done.19.refs_10_.refs_4_ = bf16[2,256,256]{2,1,0:T(8,128)(2,1)S(1)} collective-permute-done((bf16[2,256,256]{2,1,0:T(8,128)(2,1)S(1)}, bf16[2,256,256]{2,1,0:T(8,128)(2,1)S(1)}, u32[]{:S(2)}, u32[]{:S(2)}) %collective-permute-start.19) | collective-permute-done | bytes 262176 | tf_op jit(solution)/shard_map/ppermute | solution.py:424
  101.2 8.2 %shard_map.89 = (bf16[256,1024]{1,0:T(8,128)(2,1)S(1)}, bf16[2,256,1024]{2,1,0:T(8,128)(2,1)}, f32[2,256,1024]{2,1,0:T(8,128)S(1)}, bf16[2,256,1024]{2,1,0:T(8,1...) custom-call(s32[6]{0:T(128)S(1)} %stack.56.scalars, ...), custom_call_target="tpu_custom_call", output_to_operand_aliasing={{1}: (14, {})} | custom-call | flops 1275068416 | bytes 8388608 | tf_op jit(solution)/shard_map/pallas_call | solution.py:184
  109.7 2.2 %collective-permute-done.17.refs_10_.refs_4_ = bf16[2,256,256]{2,1,0:T(8,128)(2,1)S(1)} collective-permute-done((bf16[2,256,256]{2,1,0:T(8,128)(2,1)S(1)}, bf16[2,256,256]{2,1,0:T(8,128)(2,1)S(1)}, u32[]{:S(2)}, u32[]{:S(2)}) %collective-permute-start.17) | collective-permute-done | bytes 262176 | tf_op jit(solution)/shard_map/ppermute | solution.py:424
  111.9 8.0 %shard_map.90 = (bf16[256,1024]{1,0:T(8,128)(2,1)S(1)}, bf16[2,256,1024]{2,1,0:T(8,128)(2,1)}, f32[2,256,1024]{2,1,0:T(8,128)S(1)}, bf16[2,256,1024]{2,1,0:T(8,1...) custom-call(s32[6]{0:T(128)S(1)} %stack.56.scalars, ...), custom_call_target="tpu_custom_call", output_to_operand_aliasing={{0}: (14, {}), {1}: (15, {}), {2}: (16, {}), {3}: (17, {}),... | custom-call | flops 1275068416 | bytes 8388608 | tf_op jit(solution)/shard_map/pallas_call | solution.py:184
  119.9 2.5 %collective-permute-start.21 = (bf16[2,256,256]{2,1,0:T(8,128)(2,1)S(1)}, bf16[2,256,256]{2,1,0:T(8,128)(2,1)S(1)}, u32[]{:S(2)}, u32[]{:S(2)}) collective-permute-start(bf16[2,256,256]{2,1,0:T(8,128)(2,1)S(1)} %get-tuple-element.113), channel_id=1, source_target_pairs={{16,0},{18,2},{20,4},{22,6},{24,8},{26,10},{28,12},{30,14},{0,16},... | collective-permute-start | bytes 786440 | tf_op jit(solution)/shard_map/ppermute | solution.py:424
  123.7 3.1 %shard_map.88 = (bf16[256,1024]{1,0:T(8,128)(2,1)S(1)}, f32[256,1024]{1,0:T(8,128)S(1)}) custom-call(s32[6]{0:T(128)S(1)} %stack.56.scalars, bf16[256,1024]{1,0:T(8,128)(2,1)S(1)} %get-tuple-element.99.attn_ref, bf16[1024,2048]{1,0:T(8,128)(2,1)S(1)} %copy-done.1), custom_call_target="tpu_custom_call" | custom-call | flops 1073741824 | bytes 6291456 | tf_op jit(solution)/shard_map/pallas_call | solution.py:222
  129.5 7.5 %shard_map.91 = (bf16[256,1024]{1,0:T(8,128)(2,1)S(1)}, bf16[2,256,1024]{2,1,0:T(8,128)(2,1)}, f32[2,256,1024]{2,1,0:T(8,128)S(1)}, bf16[2,256,1024]{2,1,0:T(8,1...) custom-call(s32[6]{0:T(128)S(1)} %stack.56.scalars, ...), custom_call_target="tpu_custom_call", output_to_operand_aliasing={{0}: (12, {}), {1}: (13, {}), {2}: (14, {}), {3}: (15, {}),... | custom-call | flops 1275068416 | bytes 8388608 | tf_op jit(solution)/shard_map/pallas_call | solution.py:184
  137.0 7.5 %shard_map.92 = (bf16[256,1024]{1,0:T(8,128)(2,1)S(1)}, bf16[2,256,1024]{2,1,0:T(8,128)(2,1)}, f32[2,256,1024]{2,1,0:T(8,128)S(1)}, bf16[2,256,1024]{2,1,0:T(8,1...) custom-call(s32[6]{0:T(128)S(1)} %stack.56.scalars, ...), custom_call_target="tpu_custom_call", output_to_operand_aliasing={{0}: (12, {}), {1}: (13, {}), {2}: (14, {}), {3}: (15, {})} | custom-call | flops 1275068416 | bytes 8388608 | tf_op jit(solution)/shard_map/pallas_call | solution.py:184
  147.1 3.1 %shard_map.93 = (bf16[256,1024]{1,0:T(8,128)(2,1)S(1)}, f32[256,1024]{1,0:T(8,128)S(1)}) custom-call(s32[6]{0:T(128)S(1)} %stack.56.scalars, bf16[256,1024]{1,0:T(8,128)(2,1)S(1)} %get-tuple-element.125.attn_ref, bf16[1024,2048]{1,0:T(8,128)(2,1)S(1)} %copy-done.1), custom_call_target="tpu_custom_call" | custom-call | flops 1073741824 | bytes 6291456 | tf_op jit(solution)/shard_map/pallas_call | solution.py:222
  166.2 5.2 %collective-permute-done.29.refs_2_ = bf16[2,256,768]{2,1,0:T(8,128)(2,1)S(1)} collective-permute-done((bf16[2,256,768]{2,1,0:T(8,128)(2,1)S(1)}, bf16[2,256,768]{2,1,0:T(8,128)(2,1)S(1)}, u32[]{:S(2)}, u32[]{:S(2)}) %collective-permute-start.29) | collective-permute-done | bytes 786464 | tf_op jit(solution)/shard_map/ppermute | solution.py:419
  180.3 4.7 %collective-permute-done.27.refs_3_ = bf16[2,256,256]{2,1,0:T(8,128)(2,1)S(1)} collective-permute-done((bf16[2,256,256]{2,1,0:T(8,128)(2,1)S(1)}, bf16[2,256,256]{2,1,0:T(8,128)(2,1)S(1)}, u32[]{:S(2)}, u32[]{:S(2)}) %collective-permute-start.27) | collective-permute-done | bytes 262176 | tf_op jit(solution)/shard_map/ppermute | solution.py:424
  185.0 4.9 %collective-permute-done.28.refs_4_ = bf16[2,256,256]{2,1,0:T(8,128)(2,1)S(1)} collective-permute-done((bf16[2,256,256]{2,1,0:T(8,128)(2,1)S(1)}, bf16[2,256,256]{2,1,0:T(8,128)(2,1)S(1)}, u32[]{:S(2)}, u32[]{:S(2)}) %collective-permute-start.28) | collective-permute-done | bytes 262176 | tf_op jit(solution)/shard_map/ppermute | solution.py:424
  (108 shorter events, 66.2 us)
Async XLA Ops:
  2.5 40.3 %collective-permute-start.1 = (bf16[2,256,1024]{2,1,0:T(8,128)(2,1)S(1)}, bf16[2,256,1024]{2,1,0:T(8,128)(2,1)S(1)}, u32[]{:S(2)}, u32[]{:S(2)}) collective-permute-start(bf16[2,256,1024]{2,1,0:T(8,128)(2,1)S(1)} %pad_maximum_fusion), channel_id=1, source_target_pairs={{0,2},{4,6},{8,10},{12,14},{16,18},{20,22},{24,26},{28,30},{1,3},{... | collective-permute-start | bytes 3145736 | tf_op jit(solution)/shard_map/ppermute | solution.py:351
  10.5 25.5 %collective-permute-start = (bf16[1,256,1024]{2,1,0:T(8,128)(2,1)S(1)}, bf16[1,256,1024]{2,1,0:T(8,128)(2,1)S(1)}, u32[]{:S(2)}, u32[]{:S(2)}) collective-permute-start(bf16[1,256,1024]{2,1,0:T(8,128)(2,1)S(1)} %get-tuple-element.164), channel_id=1, source_target_pairs={{0,1},{1,0},{2,3},{3,2},{4,5},{5,4},{6,7},{7,6},{8,9},{9,8},{10,11... | collective-permute-start | bytes 1572872 | tf_op jit(solution)/shard_map/ppermute | solution.py:342
  13.0 49.2 %collective-permute-start.2 = (bf16[2,256,768]{2,1,0:T(8,128)(2,1)}, bf16[2,256,768]{2,1,0:T(8,128)(2,1)}, u32[]{:S(2)}, u32[]{:S(2)}) collective-permute-start(bf16[2,256,768]{2,1,0:T(8,128)(2,1)} %pad_maximum_fusion.3), channel_id=1, source_target_pairs={{0,4},{2,6},{8,12},{10,14},{16,20},{18,22},{24,28},{26,30},{1,5},{... | collective-permute-start | bytes 2359304 | tf_op jit(solution)/shard_map/ppermute | solution.py:351
  24.4 72.5 %collective-permute-start.14 = (bf16[2,256,1024]{2,1,0:T(8,128)(2,1)}, bf16[2,256,1024]{2,1,0:T(8,128)(2,1)}, u32[]{:S(2)}, u32[]{:S(2)}) collective-permute-start(bf16[2,256,1024]{2,1,0:T(8,128)(2,1)} %pad_maximum_fusion.1), channel_id=1, source_target_pairs={{0,2},{4,6},{8,10},{12,14},{16,18},{20,22},{24,26},{28,30},{1,3},{... | collective-permute-start | bytes 3145736 | tf_op jit(solution)/shard_map/ppermute | solution.py:351
  29.5 32.6 %collective-permute-start.3 = (bf16[2,256,256]{2,1,0:T(8,128)(2,1)}, bf16[2,256,256]{2,1,0:T(8,128)(2,1)}, u32[]{:S(2)}, u32[]{:S(2)}) collective-permute-start(bf16[2,256,256]{2,1,0:T(8,128)(2,1)} %pad_maximum_fusion.4), channel_id=1, source_target_pairs={{0,8},{2,10},{4,12},{6,14},{16,24},{18,26},{20,28},{22,30},{1,9},{... | collective-permute-start | bytes 786440 | tf_op jit(solution)/shard_map/ppermute | solution.py:348
  36.8 25.3 %collective-permute-start.4 = (bf16[2,256,256]{2,1,0:T(8,128)(2,1)}, bf16[2,256,256]{2,1,0:T(8,128)(2,1)}, u32[]{:S(2)}, u32[]{:S(2)}) collective-permute-start(bf16[2,256,256]{2,1,0:T(8,128)(2,1)} %pad_maximum_fusion.4), channel_id=1, source_target_pairs={{0,16},{2,18},{4,20},{6,22},{8,24},{10,26},{12,28},{14,30},{1,17},... | collective-permute-start | bytes 786440 | tf_op jit(solution)/shard_map/ppermute | solution.py:348
  43.8 55.0 %collective-permute-start.15 = (bf16[2,256,1024]{2,1,0:T(8,128)(2,1)}, bf16[2,256,1024]{2,1,0:T(8,128)(2,1)}, u32[]{:S(2)}, u32[]{:S(2)}) collective-permute-start(bf16[2,256,1024]{2,1,0:T(8,128)(2,1)} %pad_maximum_fusion.1), channel_id=1, source_target_pairs={{0,4},{2,6},{8,12},{10,14},{16,20},{18,22},{24,28},{26,30},{1,5},{... | collective-permute-start | bytes 3145736 | tf_op jit(solution)/shard_map/ppermute | solution.py:351
  62.2 33.2 %collective-permute-start.13 = (bf16[1,256,1024]{2,1,0:T(8,128)(2,1)S(1)}, bf16[1,256,1024]{2,1,0:T(8,128)(2,1)S(1)}, u32[]{:S(2)}, u32[]{:S(2)}) collective-permute-start(bf16[1,256,1024]{2,1,0:T(8,128)(2,1)S(1)} %copy-done.15), channel_id=1, source_target_pairs={{0,1},{1,0},{2,3},{3,2},{4,5},{5,4},{6,7},{7,6},{8,9},{9,8},{10,11... | collective-permute-start | bytes 1572872 | tf_op jit(solution)/shard_map/ppermute | solution.py:342
  85.4 15.8 %collective-permute-start.19 = (bf16[2,256,256]{2,1,0:T(8,128)(2,1)S(1)}, bf16[2,256,256]{2,1,0:T(8,128)(2,1)S(1)}, u32[]{:S(2)}, u32[]{:S(2)}) collective-permute-start(bf16[2,256,256]{2,1,0:T(8,128)(2,1)S(1)} %get-tuple-element.105), channel_id=1, source_target_pairs={{16,0},{18,2},{20,4},{22,6},{24,8},{26,10},{28,12},{30,14},{0,16},... | collective-permute-start | bytes 786440 | tf_op jit(solution)/shard_map/ppermute | solution.py:424
  96.9 15.0 %collective-permute-start.17 = (bf16[2,256,256]{2,1,0:T(8,128)(2,1)S(1)}, bf16[2,256,256]{2,1,0:T(8,128)(2,1)S(1)}, u32[]{:S(2)}, u32[]{:S(2)}) collective-permute-start(bf16[2,256,256]{2,1,0:T(8,128)(2,1)S(1)} %get-tuple-element.103), channel_id=1, source_target_pairs={{16,0},{18,2},{20,4},{22,6},{24,8},{26,10},{28,12},{30,14},{0,16},... | collective-permute-start | bytes 786440 | tf_op jit(solution)/shard_map/ppermute | solution.py:424
  109.4 17.4 %collective-permute-start.22 = (bf16[2,256,256]{2,1,0:T(8,128)(2,1)S(1)}, bf16[2,256,256]{2,1,0:T(8,128)(2,1)S(1)}, u32[]{:S(2)}, u32[]{:S(2)}) collective-permute-start(bf16[2,256,256]{2,1,0:T(8,128)(2,1)S(1)} %get-tuple-element.114), channel_id=1, source_target_pairs={{8,0},{10,2},{12,4},{14,6},{24,16},{26,18},{28,20},{30,22},{0,8},{... | collective-permute-start | bytes 786440 | tf_op jit(solution)/shard_map/ppermute | solution.py:424
  109.4 18.7 %collective-permute-start.23 = (bf16[2,256,256]{2,1,0:T(8,128)(2,1)S(1)}, bf16[2,256,256]{2,1,0:T(8,128)(2,1)S(1)}, u32[]{:S(2)}, u32[]{:S(2)}) collective-permute-start(bf16[2,256,256]{2,1,0:T(8,128)(2,1)S(1)} %get-tuple-element.115), channel_id=1, source_target_pairs={{16,0},{18,2},{20,4},{22,6},{24,8},{26,10},{28,12},{30,14},{0,16},... | collective-permute-start | bytes 786440 | tf_op jit(solution)/shard_map/ppermute | solution.py:424
  119.9 17.1 %collective-permute-start.20 = (bf16[2,256,256]{2,1,0:T(8,128)(2,1)S(1)}, bf16[2,256,256]{2,1,0:T(8,128)(2,1)S(1)}, u32[]{:S(2)}, u32[]{:S(2)}) collective-permute-start(bf16[2,256,256]{2,1,0:T(8,128)(2,1)S(1)} %get-tuple-element.112), channel_id=1, source_target_pairs={{8,0},{10,2},{12,4},{14,6},{24,16},{26,18},{28,20},{30,22},{0,8},{... | collective-permute-start | bytes 786440 | tf_op jit(solution)/shard_map/ppermute | solution.py:424
  119.9 17.1 %collective-permute-start.21 = (bf16[2,256,256]{2,1,0:T(8,128)(2,1)S(1)}, bf16[2,256,256]{2,1,0:T(8,128)(2,1)S(1)}, u32[]{:S(2)}, u32[]{:S(2)}) collective-permute-start(bf16[2,256,256]{2,1,0:T(8,128)(2,1)S(1)} %get-tuple-element.113), channel_id=1, source_target_pairs={{16,0},{18,2},{20,4},{22,6},{24,8},{26,10},{28,12},{30,14},{0,16},... | collective-permute-start | bytes 786440 | tf_op jit(solution)/shard_map/ppermute | solution.py:424
  122.4 28.7 %collective-permute-start.32 = (bf16[2,256,1024]{2,1,0:T(8,128)(2,1)S(1)}, bf16[2,256,1024]{2,1,0:T(8,128)(2,1)S(1)}, u32[]{:S(2)}, u32[]{:S(2)}) collective-permute-start(bf16[2,256,1024]{2,1,0:T(8,128)(2,1)S(1)} %get-tuple-element.138), channel_id=1, source_target_pairs={{2,0},{6,4},{10,8},{14,12},{18,16},{22,20},{26,24},{30,28},{3,1},{... | collective-permute-start | bytes 3145736 | tf_op jit(solution)/shard_map/ppermute | solution.py:419
  126.8 27.7 %collective-permute-start.33 = (bf16[2,256,1024]{2,1,0:T(8,128)(2,1)S(1)}, bf16[2,256,1024]{2,1,0:T(8,128)(2,1)S(1)}, u32[]{:S(2)}, u32[]{:S(2)}) collective-permute-start(bf16[2,256,1024]{2,1,0:T(8,128)(2,1)S(1)} %get-tuple-element.139), channel_id=1, source_target_pairs={{4,0},{6,2},{12,8},{14,10},{20,16},{22,18},{28,24},{30,26},{5,1},{... | collective-permute-start | bytes 3145736 | tf_op jit(solution)/shard_map/ppermute | solution.py:419
  128.1 22.1 %collective-permute-start.12 = (bf16[256,1024]{1,0:T(8,128)(2,1)S(1)}, bf16[256,1024]{1,0:T(8,128)(2,1)S(1)}, u32[]{:S(2)}, u32[]{:S(2)}) collective-permute-start(bf16[256,1024]{1,0:T(8,128)(2,1)S(1)} %get-tuple-element.101), channel_id=1, source_target_pairs={{0,1},{1,0},{2,3},{3,2},{4,5},{5,4},{6,7},{7,6},{8,9},{9,8},{10,11... | collective-permute-start | bytes 1572872 | tf_op jit(solution)/shard_map/ppermute | solution.py:342
  144.6 28.1 %collective-permute-start.25 = (bf16[2,256,1024]{2,1,0:T(8,128)(2,1)S(1)}, bf16[2,256,1024]{2,1,0:T(8,128)(2,1)S(1)}, u32[]{:S(2)}, u32[]{:S(2)}) collective-permute-start(bf16[2,256,1024]{2,1,0:T(8,128)(2,1)S(1)} %get-tuple-element.130), channel_id=1, source_target_pairs={{2,0},{6,4},{10,8},{14,12},{18,16},{22,20},{26,24},{30,28},{3,1},{... | collective-permute-start | bytes 3145736 | tf_op jit(solution)/shard_map/ppermute | solution.py:419
  145.8 25.5 %collective-permute-start.29 = (bf16[2,256,768]{2,1,0:T(8,128)(2,1)S(1)}, bf16[2,256,768]{2,1,0:T(8,128)(2,1)S(1)}, u32[]{:S(2)}, u32[]{:S(2)}) collective-permute-start(bf16[2,256,768]{2,1,0:T(8,128)(2,1)S(1)} %get-tuple-element.134), channel_id=1, source_target_pairs={{4,0},{6,2},{12,8},{14,10},{20,16},{22,18},{28,24},{30,26},{5,1},{... | collective-permute-start | bytes 2359304 | tf_op jit(solution)/shard_map/ppermute | solution.py:419
  150.2 14.6 %collective-permute-start.24 = (bf16[256,1024]{1,0:T(8,128)(2,1)S(1)}, bf16[256,1024]{1,0:T(8,128)(2,1)S(1)}, u32[]{:S(2)}, u32[]{:S(2)}) collective-permute-start(bf16[256,1024]{1,0:T(8,128)(2,1)S(1)} %get-tuple-element.127), channel_id=1, source_target_pairs={{0,1},{1,0},{2,3},{3,2},{4,5},{5,4},{6,7},{7,6},{8,9},{9,8},{10,11... | collective-permute-start | bytes 1572872 | tf_op jit(solution)/shard_map/ppermute | solution.py:342
  151.2 27.4 %collective-permute-start.30 = (bf16[2,256,256]{2,1,0:T(8,128)(2,1)S(1)}, bf16[2,256,256]{2,1,0:T(8,128)(2,1)S(1)}, u32[]{:S(2)}, u32[]{:S(2)}) collective-permute-start(bf16[2,256,256]{2,1,0:T(8,128)(2,1)S(1)} %get-tuple-element.135), channel_id=1, source_target_pairs={{8,0},{10,2},{12,4},{14,6},{24,16},{26,18},{28,20},{30,22},{9,1},{... | collective-permute-start | bytes 786440 | tf_op jit(solution)/shard_map/ppermute | solution.py:424
  154.5 24.1 %collective-permute-start.31 = (bf16[2,256,256]{2,1,0:T(8,128)(2,1)S(1)}, bf16[2,256,256]{2,1,0:T(8,128)(2,1)S(1)}, u32[]{:S(2)}, u32[]{:S(2)}) collective-permute-start(bf16[2,256,256]{2,1,0:T(8,128)(2,1)S(1)} %get-tuple-element.136), channel_id=1, source_target_pairs={{16,0},{18,2},{20,4},{22,6},{24,8},{26,10},{28,12},{30,14},{17,1},... | collective-permute-start | bytes 786440 | tf_op jit(solution)/shard_map/ppermute | solution.py:424
  164.9 15.4 %collective-permute-start.26 = (bf16[2,256,256]{2,1,0:T(8,128)(2,1)S(1)}, bf16[2,256,256]{2,1,0:T(8,128)(2,1)S(1)}, u32[]{:S(2)}, u32[]{:S(2)}) collective-permute-start(bf16[2,256,256]{2,1,0:T(8,128)(2,1)S(1)} %get-tuple-element.131), channel_id=1, source_target_pairs={{4,0},{6,2},{12,8},{14,10},{20,16},{22,18},{28,24},{30,26},{5,1},{... | collective-permute-start | bytes 786440 | tf_op jit(solution)/shard_map/ppermute | solution.py:419
  172.7 17.2 %collective-permute-start.28 = (bf16[2,256,256]{2,1,0:T(8,128)(2,1)S(1)}, bf16[2,256,256]{2,1,0:T(8,128)(2,1)S(1)}, u32[]{:S(2)}, u32[]{:S(2)}) collective-permute-start(bf16[2,256,256]{2,1,0:T(8,128)(2,1)S(1)} %get-tuple-element.133), channel_id=1, source_target_pairs={{16,0},{18,2},{20,4},{22,6},{24,8},{26,10},{28,12},{30,14},{17,1},... | collective-permute-start | bytes 786440 | tf_op jit(solution)/shard_map/ppermute | solution.py:424
  (26 other events, 197.8 us)

commit v2 on v1

v2 whole, which is shorter than its diff:
```python
from functools import partial

import jax
import jax.numpy as jnp
from jax import lax
from jax.experimental import pallas as pl
from jax.experimental.pallas import tpu as pltpu
from jax.sharding import PartitionSpec as P

HEAD_DIM = 128
COARSE_LEVELS = 2
LOG2_E = 1.4426950408889634
FAR_OFF = 1e30
VMEM_LIMIT = 24 * 1024 * 1024
COST_SHARE = 20


def cost(flops, bytes_accessed, transcendentals=0):
    parts = (flops, bytes_accessed, transcendentals)
    flops, bytes_accessed, transcendentals = (int(part * COST_SHARE) for part in parts)
    return pl.CostEstimate(
        flops=flops, bytes_accessed=bytes_accessed, transcendentals=transcendentals
    )


def dot_t(a, b):
    return lax.dot_general(a, b, (((1,), (1,)), ((), ())), preferred_element_type=jnp.float32)


def dot_n(a, b):
    return lax.dot_general(a, b, (((1,), (0,)), ((), ())), preferred_element_type=jnp.float32)


def dot_l(a, b):
    return lax.dot_general(a, b, (((0,), (0,)), ((), ())), preferred_element_type=jnp.float32)


def unit_steps(levels, width, refs, masks, scratch, place):
    q_ref, k_ref, v_ref, grad_ref, far_refs, attn_ref, dq_ref, own_ref, out_refs = refs
    keys_scr, values_scr, weight_scr, low_scr, grad_scr = [ref.at[place] for ref in scratch]
    cols = slice(place * HEAD_DIM, (place + 1) * HEAD_DIM)
    scale = HEAD_DIM ** (-0.5)
    rows = q_ref.shape[1]
    blocks = range(levels + 1)

    def span(index):
        return pl.ds(index * rows, rows)

    for index in blocks:
        keys_scr[span(index), :] = k_ref[0, :, cols] if index == 0 else far_refs[index - 1][0, :, cols]
        values_scr[span(index), :] = v_ref[0, :, cols] if index == 0 else far_refs[index - 1][1, :, cols]
    queries = q_ref[0, :, cols]
    queries_t = queries.astype(jnp.float32).T.astype(jnp.bfloat16)
    weight_scr[...] = dot_n(keys_scr[...], queries_t)
    yield
    grad_t = grad_ref[cols, :]
    grad = grad_t.astype(jnp.float32).T.astype(jnp.bfloat16)
    factor = jnp.float32(scale * LOG2_E)
    own_scores = weight_scr[span(0), :]
    key_at = lax.broadcasted_iota(jnp.int32, own_scores.shape, 0)
    query_at = lax.broadcasted_iota(jnp.int32, own_scores.shape, 1)
    weight_scr[span(0), :] = jnp.where(key_at <= query_at, own_scores, -jnp.float32(FAR_OFF))
    maxima = None
    for index in blocks:
        top = jnp.max(weight_scr[span(index), :], axis=0, keepdims=True) * factor - masks[index]
        maxima = top if maxima is None else jnp.maximum(maxima, top)
    total = None
    for index in blocks:
        powers = jnp.exp2(weight_scr[span(index), :] * factor - (maxima + masks[index]))
        weight_scr[span(index), :] = powers
        part = jnp.sum(powers, axis=0, keepdims=True)
        total = part if total is None else total + part
    inverse = 1.0 / total
    for index in blocks:
        weights = weight_scr[span(index), :] * inverse
        weight_scr[span(index), :] = weights
        low_scr[span(index), :] = weights.astype(jnp.bfloat16)
    yield
    attn_t = dot_l(values_scr[...], low_scr[...])
    grad_weights = dot_n(values_scr[...], grad_t)
    value_terms = dot_n(low_scr[...], grad)
    yield
    attn_t = attn_t.astype(jnp.bfloat16).astype(jnp.float32)
    attn_ref[:, cols] = attn_t.T.astype(jnp.bfloat16)
    row_dsum = jnp.sum(grad_t.astype(jnp.float32) * attn_t, axis=0, keepdims=True)
    own_ref[1, :, cols] = value_terms[:rows]
    for index in blocks:
        if index:
            out_refs[index - 1][1, :, cols] = value_terms[index * rows : (index + 1) * rows].astype(
                jnp.bfloat16
            )
    for index in blocks:
        grad_scr[span(index), :] = (
            weight_scr[span(index), :]
            * (grad_weights[index * rows : (index + 1) * rows] - row_dsum)
        ).astype(jnp.bfloat16)
    yield
    key_terms = dot_n(grad_scr[...], queries)
    dq_t = dot_l(keys_scr[...], grad_scr[...])
    yield
    own_ref[0, :, cols] = key_terms[:rows] * scale
    for index in blocks:
        if index:
            out_refs[index - 1][0, :, cols] = (
                key_terms[index * rows : (index + 1) * rows] * scale
            ).astype(jnp.bfloat16)
    dq_ref[0, :, cols] = (dq_t * scale).T.astype(jnp.bfloat16)
    yield


def unit_kernel(levels, fine, coarse, has_next, n_alias, pair, scalars, *refs):
    refs = list(refs)
    inputs, refs = refs[:4], refs[4:]
    far_refs, refs = refs[:levels], refs[levels:]
    if has_next:
        (next_k, next_v), refs = refs[:2], refs[2:]
    refs = refs[n_alias:]
    outputs, refs = refs[:3], refs[3:]
    coarse_refs, refs = refs[: len(coarse)], refs[len(coarse) :]
    fine_refs, scratch = refs[: len(fine)], refs[len(fine) :]
    out_refs = [
        coarse_refs[coarse.index(level)] if level in coarse else fine_refs[fine.index(level)]
        for level in range(levels)
    ]
    masks = [jnp.float32(0.0)] + [
        jnp.where(scalars[2 + level] == 1, jnp.float32(0.0), jnp.float32(FAR_OFF))
        for level in range(levels)
    ]
    steps = [
        unit_steps(levels, pair, (*inputs, far_refs, *outputs, out_refs), masks, scratch, place)
        for place in range(pair)
    ]
    for tick in range(6 + pair - 1):
        for place, step in enumerate(steps):
            if 0 <= tick - place < 6:
                next(step)
    if has_next:
        for level in fine:

            @pl.when(scalars[2 + level] == 0)
            def _():
                out_refs[level][0] = next_k[0]
                out_refs[level][1] = next_v[0]


def chunk_call(levels, fine, coarse, chunk, upcoming, far_at, down_at, down_units, scalars, arrays, far, carried, gates):
    queries, keys, values, attn_grad = arrays
    batch_at, head_at, count = chunk
    rows, width = queries.shape[1], queries.shape[2]
    has_next = upcoming is not None
    pair = 2 if count % 2 == 0 else 1
    head_at //= pair
    far_at = [at // pair for at in far_at]
    down_at = [at // pair for at in down_at]
    cols = pair * HEAD_DIM

    def of_unit(batch, head):
        return pl.BlockSpec((1, rows, cols), lambda i, s, b=batch, h=head: (b, 0, h + i))

    in_specs = [
        of_unit(batch_at, head_at),
        of_unit(batch_at, head_at),
        of_unit(batch_at, head_at),
        pl.BlockSpec((cols, rows), lambda i, s: (head_at + i, 0)),
    ]
    operands = [queries, keys, values, attn_grad]
    for level in range(levels):
        in_specs.append(
            pl.BlockSpec((2, rows, cols), lambda i, s, h=far_at[level]: (0, 0, h + i))
        )
        operands.append(far[level])
    if has_next:
        in_specs += [of_unit(upcoming[0], upcoming[1] // pair)] * 2
        operands += [keys, values]

    out_shapes = [
        jax.ShapeDtypeStruct((rows, width), jnp.bfloat16),
        jax.ShapeDtypeStruct(queries.shape, jnp.bfloat16),
        jax.ShapeDtypeStruct((2, rows, width), jnp.float32),
    ]
    out_specs = [
        pl.BlockSpec((rows, cols), lambda i, s: (0, head_at + i)),
        of_unit(batch_at, head_at),
        pl.BlockSpec((2, rows, cols), lambda i, s: (0, 0, head_at + i)),
    ]
    for place, level in enumerate(coarse):
        out_shapes.append(
            jax.ShapeDtypeStruct((2, rows, down_units[place] * HEAD_DIM), jnp.bfloat16)
        )
        out_specs.append(
            pl.BlockSpec((2, rows, cols), lambda i, s, h=down_at[place]: (0, 0, h + i))
        )
    for level in fine:
        out_shapes.append(jax.ShapeDtypeStruct((2, rows, count * HEAD_DIM), jnp.bfloat16))
        out_specs.append(pl.BlockSpec((2, rows, cols), lambda i, s: (0, 0, i)))

    aliases = {}
    for place, held in enumerate(carried):
        if held is not None:
            aliases[1 + len(operands)] = place
            in_specs.append(pl.BlockSpec(memory_space=pl.ANY))
            operands.append(held)
    for gate in gates:
        in_specs.append(pl.BlockSpec(memory_space=pl.ANY))
        operands.append(gate)
    seen = (levels + 1) * rows
    flops = count * 2 * 6 * seen * rows * HEAD_DIM
    return pl.pallas_call(
        partial(unit_kernel, levels, fine, coarse, has_next, len(aliases) + len(gates), pair),
        out_shape=out_shapes,
        grid_spec=pltpu.PrefetchScalarGridSpec(
            num_scalar_prefetch=1,
            grid=(count // pair,),
            in_specs=in_specs,
            out_specs=out_specs,
            scratch_shapes=[
                pltpu.VMEM((pair, seen, HEAD_DIM), jnp.bfloat16),
                pltpu.VMEM((pair, seen, HEAD_DIM), jnp.bfloat16),
                pltpu.VMEM((pair, seen, rows), jnp.float32),
                pltpu.VMEM((pair, seen, rows), jnp.bfloat16),
                pltpu.VMEM((pair, seen, rows), jnp.bfloat16),
            ],
        ),
        input_output_aliases=aliases,
        compiler_params=pltpu.CompilerParams(vmem_limit_bytes=VMEM_LIMIT),
        cost_estimate=cost(
            flops=flops, bytes_accessed=count * 4 * 2**20, transcendentals=count * seen * rows
        ),
    )(scalars, *operands)


def grad_kernel(scalars, own_ref, other_ref, proj_own, proj_other, grad_ref):
    grad_ref[...] = (
        dot_t(proj_own[...], own_ref[0]) + dot_t(proj_other[...], other_ref[0])
    ).astype(jnp.bfloat16)


def grad_project(scalars, output_grad, batch_at, other_grad, out_proj):
    rows = output_grad.shape[1]
    width, wide = out_proj.shape[0], out_proj.shape[1] // 2
    block = 256
    return pl.pallas_call(
        grad_kernel,
        out_shape=jax.ShapeDtypeStruct((width, rows), jnp.bfloat16),
        grid_spec=pltpu.PrefetchScalarGridSpec(
            num_scalar_prefetch=1,
            grid=(width // block,),
            in_specs=[
                pl.BlockSpec((1, rows, wide), lambda i, s: (batch_at, 0, 0)),
                pl.BlockSpec((1, rows, wide), lambda i, s: (0, 0, 0)),
                pl.BlockSpec((block, wide), lambda i, s: (i, s[0])),
                pl.BlockSpec((block, wide), lambda i, s: (i, s[1])),
            ],
            out_specs=pl.BlockSpec((block, rows), lambda i, s: (i, 0)),
        ),
        compiler_params=pltpu.CompilerParams(vmem_limit_bytes=VMEM_LIMIT),
        cost_estimate=cost(
            flops=4 * rows * wide * width, bytes_accessed=6 * 2**20, transcendentals=0
        ),
    )(scalars, output_grad, other_grad, out_proj, out_proj)


def project_kernel(scalars, attn_ref, proj_ref, send_ref, own_ref):
    step = pl.program_id(0)
    product = dot_n(attn_ref[...], proj_ref[...])

    @pl.when(step < 2)
    def _():
        send_ref[...] = product.astype(jnp.bfloat16)

    @pl.when(step >= 2)
    def _():
        own_ref[...] = product


def project(scalars, attn, out_proj):
    rows, depth = attn.shape
    wide = out_proj.shape[1] // 2
    block = wide // 2
    return pl.pallas_call(
        project_kernel,
        out_shape=[
            jax.ShapeDtypeStruct((rows, wide), jnp.bfloat16),
            jax.ShapeDtypeStruct((rows, wide), jnp.float32),
        ],
        grid_spec=pltpu.PrefetchScalarGridSpec(
            num_scalar_prefetch=1,
            grid=(4,),
            in_specs=[
                pl.BlockSpec((rows, depth), lambda i, s: (0, 0)),
                pl.BlockSpec(
                    (depth, block), lambda i, s: (0, jnp.where(i < 2, s[1], s[0]) * 2 + i % 2)
                ),
            ],
            out_specs=[
                pl.BlockSpec((rows, block), lambda i, s: (0, jnp.minimum(i, 1))),
                pl.BlockSpec((rows, block), lambda i, s: (0, jnp.maximum(i - 2, 0))),
            ],
        ),
        compiler_params=pltpu.CompilerParams(vmem_limit_bytes=VMEM_LIMIT),
        cost_estimate=cost(
            flops=4 * rows * depth * wide, bytes_accessed=6 * 2**20, transcendentals=0
        ),
    )(scalars, attn, out_proj)


def finish_kernel(levels, masked, scalars, *refs):
    own_ref, far_refs = refs[0], refs[1 : 1 + levels * len(masked)]
    key_ref, value_ref = refs[-2:]
    for index, skip in enumerate(masked):
        wide = far_refs[index * levels].shape[2]
        cols = slice(index * wide, (index + 1) * wide)
        for place, target in enumerate((key_ref, value_ref)):
            total = own_ref[place, :, cols]
            for level in range(levels):
                term = far_refs[index * levels + level][place].astype(jnp.float32)
                if skip[level]:
                    term = jnp.where(scalars[2 + level] == 1, jnp.zeros_like(term), term)
                total = total + term
            target[0, :, cols] = total.astype(jnp.bfloat16)


def finish(levels, masked, chunks, far_at, shape, scalars, own, far, carried):
    batch_at, head_at, count = chunks[0]
    rows, cols, wide = shape[1], count * HEAD_DIM, len(chunks) * count * HEAD_DIM
    at = head_at * HEAD_DIM // wide
    in_specs = [pl.BlockSpec((2, rows, wide), lambda i, s: (0, 0, at))]
    operands = [own]
    for index in range(len(chunks)):
        for level in range(levels):
            in_specs.append(
                pl.BlockSpec(
                    (2, rows, cols), lambda i, s, h=far_at[index][level] // count: (0, 0, h)
                )
            )
            operands.append(far[index][level])
    aliases = {}
    for place, held in enumerate(carried):
        if held is not None:
            aliases[1 + len(operands)] = place
            in_specs.append(pl.BlockSpec(memory_space=pl.ANY))
            operands.append(held)
    out_spec = pl.BlockSpec((1, rows, wide), lambda i, s: (batch_at, 0, at))
    return pl.pallas_call(
        partial(finish_kernel, levels, masked),
        out_shape=[jax.ShapeDtypeStruct(shape, jnp.bfloat16)] * 2,
        grid_spec=pltpu.PrefetchScalarGridSpec(
            num_scalar_prefetch=1, grid=(1,), in_specs=in_specs, out_specs=[out_spec] * 2
        ),
        input_output_aliases=aliases,
        compiler_params=pltpu.CompilerParams(vmem_limit_bytes=VMEM_LIMIT),
        cost_estimate=cost(
            flops=2 * (levels + 1) * rows * wide,
            bytes_accessed=rows * wide * 4 * (levels + 3),
            transcendentals=0,
        ),
    )(scalars, *operands)


def groups_of(sizes):
    return [(sum(sizes[:index]), size) for index, size in enumerate(sizes)]


def holder(groups, first):
    for index, (start, size) in enumerate(groups):
        if start <= first < start + size:
            return index, first - start
    raise ValueError("unit")


def body(queries, key_states, value_states, output_grad, out_proj):
    batch, rows, width = queries.shape
    heads = width // HEAD_DIM
    seq_size = lax.axis_size("seq")
    levels = seq_size.bit_length() - 1
    coarse = list(range(min(COARSE_LEVELS, levels)))
    fine = list(range(len(coarse), levels))
    place = lax.axis_index("seq")
    half = lax.axis_index("head")
    scalars = jnp.stack(
        [half, 1 - half] + [place // 2**level % 2 for level in range(levels)]
    ).astype(jnp.int32)

    step = 2
    units = batch * heads
    count = units // step
    chunks = [(t * step // heads, t * step % heads, step) for t in range(count)]
    ups = [groups_of([units]), groups_of([heads] * batch)]
    downs = [
        groups_of([units]),
        groups_of([heads] * (batch - 1) + [2 * step] * (heads // (2 * step))),
    ]

    lower = [[i for i in range(seq_size) if not (i >> level) & 1] for level in range(levels)]
    up_pairs = [[(i, i + 2**level) for i in lower[level]] for level in range(levels)]
    down_pairs = [[(i + 2**level, i) for i in lower[level]] for level in range(levels)]

    def behind(source, *earlier):
        earlier = [item for item in earlier if item is not None]
        return lax.optimization_barrier((source, *earlier))[0] if earlier else source

    def packed(group, *earlier):
        first, last = group[0], group[0] + group[1]
        sources = behind((key_states, value_states), *earlier)
        spans = []
        for at in range(batch):
            low, high = max(first, at * heads), min(last, (at + 1) * heads)
            if low < high:
                spans.append((at, (low - at * heads) * HEAD_DIM, (high - at * heads) * HEAD_DIM))
        return jnp.stack(
            [
                jnp.concatenate([source[at, :, low:high] for at, low, high in spans], axis=1)
                for source in sources
            ]
        )

    def other_half(source):
        return lax.ppermute(source, "head", [(0, 1), (1, 0)])

    far_fine, far_coarse = {}, {}

    def send_coarse(level, index, *earlier):
        far_coarse[level, index] = lax.ppermute(
            packed(ups[level][index], *earlier), "seq", up_pairs[level]
        )

    def send_grad(at, *earlier):
        other = other_half(behind(output_grad, *earlier)[at : at + 1])
        attn_grads[at] = grad_project(scalars, output_grad, at, other, out_proj)
        return other

    def arrived(t):
        return [far_fine[level, t] for level in fine]

    attn_grads, gates = {}, {}
    opening = packed((0, 2 * step))
    for level in reversed(fine):
        far_fine[level, 0] = far_fine[level, 1] = lax.ppermute(opening, "seq", up_pairs[level])
    for level in reversed(coarse):
        send_coarse(level, 0)
    first_grad = send_grad(0)
    send_grad(1, first_grad)
    gates[3] = (attn_grads[1],)

    attn = [None] * batch
    own = [None] * batch
    query_grad = None
    down_buffers = {}
    back_coarse = {}
    grads = (None, None)

    def finished(first, last, grads):
        far, far_at, masked = [], [], []
        for c in range(first, last):
            chunk = chunks[c]
            far.append([])
            far_at.append([])
            masked.append([])
            for level in range(levels):
                if level in coarse:
                    index, at = holder(downs[level], c * step)
                    far[-1].append(back_coarse[level, index])
                    masked[-1].append(False)
                else:
                    far[-1].append(far_fine[level, c + 2])
                    at = 0
                    masked[-1].append(c + 2 < count)
                far_at[-1].append(at)
        return finish(
            levels,
            masked,
            chunks[first:last],
            far_at,
            queries.shape,
            scalars,
            own[chunks[first][0]],
            far,
            grads,
        )

    def send_down(level, index, *earlier):
        back_coarse[level, index] = lax.ppermute(
            behind(down_buffers[level, index], *earlier), "seq", down_pairs[level]
        )

    def send_out(*earlier):
        parts = [project(scalars, source, out_proj) for source in attn]
        sent = behind(jnp.stack([send for send, _ in parts]), *earlier)
        kept = jnp.stack([kept for _, kept in parts])
        return kept, other_half(sent)

    for t, chunk in enumerate(chunks):
        at = chunk[0]
        upcoming = chunks[t + 2] if t + 2 < count else None
        far, far_at, down_at, down_units, down_index = [], [], [], [], []
        for level in range(levels):
            if level in coarse:
                index, offset = holder(ups[level], t * step)
                far.append(far_coarse[level, index])
                index, down_offset = holder(downs[level], t * step)
                down_index.append(index)
                down_at.append(down_offset)
                down_units.append(downs[level][index][1])
            else:
                far.append(far_fine[level, t])
                offset = t * step if t < 2 else 0
            far_at.append(offset)
        carried = [attn[at], query_grad, own[at]] + [
            down_buffers.get((level, down_index[level])) for level in coarse
        ]
        results = chunk_call(
            levels,
            fine,
            coarse,
            chunk,
            upcoming,
            far_at,
            down_at,
            down_units,
            scalars,
            (queries, key_states, value_states, attn_grads[at]),
            far,
            carried,
            gates.get(t, ()),
        )
        attn[at], query_grad, own[at] = results[:3]
        for place_of, level in reversed(list(enumerate(fine))):
            pairs = down_pairs[level] + (up_pairs[level] if upcoming is not None else [])
            far_fine[level, t + 2] = lax.ppermute(results[3 + len(coarse) + place_of], "seq", pairs)
        for level in coarse:
            down_buffers[level, down_index[level]] = results[3 + level]
        marker = results[-1]
        if t == 0:
            send_coarse(1, 1, marker)
        if t == 3:
            send_down(1, 0)
            gates[6] = (back_coarse[1, 0],)
        if t == 5:
            send_down(1, 1, back_coarse[1, 0])
            gates[7] = (back_coarse[1, 1],)
    last = arrived(count)
    send_down(1, 2, back_coarse[1, 1], *last)
    kept, received = send_out(*last)
    send_down(0, 0, *last)
    grads = finished(0, 4, grads)
    grads = finished(4, 7, grads)
    grads = finished(7, 8, grads)
    received = behind(received, *grads)
    layer_out = (kept + received.astype(jnp.float32)).astype(jnp.bfloat16)
    return layer_out, query_grad, grads[0], grads[1]


def solution(mesh):
    spec = P(None, "seq", "head")
    return jax.shard_map(
        body,
        mesh=mesh,
        in_specs=(spec, spec, spec, spec, P("head", None)),
        out_specs=(spec, spec, spec, spec),
        check_vma=False,
    )
```

time: 192 us -> 166 us (0.86)
  Pallas kernels: 83.3 us -> 61.6 us
  waiting for transfers between devices: 26.5 us -> 43.6 us
  starting transfers between devices: 63.7 us -> 47.6 us
  local copies, waits for them, and re-layouts: 12.9 us -> 6.58 us
    pallas_call x8, Pallas kernels: 63.3 us -> 43.2 us  [chunk_call(): pl.pallas_call(partial(unit_kernel, levels, fine, coarse, has_next, len(a...]
    ppermute x14 -> x9, starting transfers between devices: 41.5 us -> 28 us  [the longest x3 11.6 us: send_coarse(): lax.ppermute(packed(ups[level][index], *earlier), 'seq', up_pairs[level])]
    ppermute x14 -> x9, waiting for transfers between devices: 8.79 us -> 20.9 us  [the longest x4 18.1 us: send_down(): lax.ppermute(behind(down_buffers[level, index], *earlier), 'seq', down_pa...]
    pallas_call x8 -> x3, Pallas kernels: 13.9 us -> 5.34 us  [finish(): pl.pallas_call(partial(finish_kernel, levels, masked), out_shape=[jax.Sha...]
    unnamed x32 -> x12, local copies, waits for them, and re-layouts: 10.1 us -> 2.21 us
    ppermute x4 -> x3, waiting for transfers between devices: 1.93 us -> 9.56 us  [other_half(): return lax.ppermute(source, 'head', [(0, 1), (1, 0)])]
    pallas_call x0 -> x2, Pallas kernels: none -> 6.9 us  [grad_project(): pl.pallas_call(grad_kernel, out_shape=jax.ShapeDtypeStruct((width, rows),...]
    ppermute x16, waiting for transfers between devices: 15.7 us -> 13.1 us  [body(): lax.ppermute(results[3 + len(coarse) + place_of], 'seq', pairs)]
  transfers between devices with their start and end apart: 34 -> 28, of which waited for: 11 -> 15; matrix products, arithmetic and copies ran while one was open for 3% -> 3% of each run, Pallas kernels for 43% -> 34%
where the time goes in v2:
time: 166 us; the launch traced here: 165 us
  Pallas kernels  61.6 us (37%)
  starting transfers between devices  47.6 us (29%)
  waiting for transfers between devices  43.6 us (26%)
  local copies, waits for them, and re-layouts  6.58 us (4%)
  other arithmetic  5.15 us (3%)
    pallas_call x8, Pallas kernels, chunk_call(): pl.pallas_call(partial(unit_kernel, levels, fine, coarse, has_next, len(a...  43.2 us
    ppermute x4, waiting for transfers between devices, send_down(): lax.ppermute(behind(down_buffers[level, index], *earlier), 'seq', down_pa...  18.1 us
    ppermute x16, starting transfers between devices, body(): lax.ppermute(results[3 + len(coarse) + place_of], 'seq', pairs)  16 us
    ppermute x16, waiting for transfers between devices, body(): lax.ppermute(results[3 + len(coarse) + place_of], 'seq', pairs)  13.1 us
    ppermute x3, starting transfers between devices, send_coarse(): lax.ppermute(packed(ups[level][index], *earlier), 'seq', up_pairs[level])  11.6 us
    ppermute x2, starting transfers between devices, body(): lax.ppermute(opening, 'seq', up_pairs[level])  11 us
    ppermute x3, waiting for transfers between devices, other_half(): return lax.ppermute(source, 'head', [(0, 1), (1, 0)])  9.56 us
    pallas_call x2, Pallas kernels, grad_project(): pl.pallas_call(grad_kernel, out_shape=jax.ShapeDtypeStruct((width, rows),...  6.9 us
  transfers between devices with their start and end apart: 28, of which 15 were waited for; matrix products, arithmetic and copies ran while one was open for 3% of the time, Pallas kernels for 34%

profile of v2, /device:TPU:0, one launch (start us, length us, event | category | flops | bytes accessed | tf_op | source)
XLA Modules:
  0.0 165.4 jit_solution(16847193900937945815)
XLA Ops:
  3.5 5.7 %collective-permute-start.3 = (bf16[2,256,512]{2,1,0:T(8,128)(2,1)}, bf16[2,256,512]{2,1,0:T(8,128)(2,1)}, u32[]{:S(2)}, u32[]{:S(2)}) collective-permute-start(bf16[2,256,512]{2,1,0:T(8,128)(2,1)} %pad_maximum_fusion.4), channel_id=1, source_target_pairs={{0,8},{2,10},{4,12},{6,14},{16,24},{18,26},{20,28},{22,30},{1,9},{... | collective-permute-start | bytes 1572872 | tf_op jit(solution)/shard_map/ppermute | solution.py:438
  9.3 5.3 %collective-permute-start.4 = (bf16[2,256,512]{2,1,0:T(8,128)(2,1)}, bf16[2,256,512]{2,1,0:T(8,128)(2,1)}, u32[]{:S(2)}, u32[]{:S(2)}) collective-permute-start(bf16[2,256,512]{2,1,0:T(8,128)(2,1)} %pad_maximum_fusion.4), channel_id=1, source_target_pairs={{0,16},{2,18},{4,20},{6,22},{8,24},{10,26},{12,28},{14,30},{1,17},... | collective-permute-start | bytes 1572872 | tf_op jit(solution)/shard_map/ppermute | solution.py:438
  20.0 2.7 %collective-permute-start.1 = (bf16[2,256,2048]{2,1,0:T(8,128)(2,1)}, bf16[2,256,2048]{2,1,0:T(8,128)(2,1)}, u32[]{:S(2)}, u32[]{:S(2)}) collective-permute-start(bf16[2,256,2048]{2,1,0:T(8,128)(2,1)} %pad_maximum_fusion), channel_id=1, source_target_pairs={{0,2},{4,6},{8,10},{12,14},{16,18},{20,22},{24,26},{28,30},{1,3},{... | collective-permute-start | bytes 6291464 | tf_op jit(solution)/shard_map/ppermute | solution.py:423
  23.8 4.4 %collective-permute-start.2 = (bf16[2,256,1024]{2,1,0:T(8,128)(2,1)}, bf16[2,256,1024]{2,1,0:T(8,128)(2,1)}, u32[]{:S(2)}, u32[]{:S(2)}) collective-permute-start(bf16[2,256,1024]{2,1,0:T(8,128)(2,1)} %pad_maximum_fusion.1), channel_id=1, source_target_pairs={{0,4},{2,6},{8,12},{10,14},{16,20},{18,22},{24,28},{26,30},{1,5},{... | collective-permute-start | bytes 3145736 | tf_op jit(solution)/shard_map/ppermute | solution.py:423
  33.6 4.1 %shard_map.84.refs_3_ = bf16[1024,256]{1,0:T(8,128)(2,1)S(1)} custom-call(s32[6]{0:T(128)S(1)} %stack.63.scalars, bf16[2,256,1024]{2,1,0:T(8,128)(2,1)S(1)} %copy-done.2, bf16[1,256,1024]{2,1,0:T(8,128)(2,1)} %collective-permute-done.other_ref, bf16[1024,2048]{1,0:T(8,128)(2,1)S(1)} %copy-done.3, bf16[1024,2048]{1,0:T(8,128)(2,1)S(1)} %copy-done.3), custom_call_target="tpu_custom_call" | custom-call | flops 21474836480 | bytes 125829120 | tf_op jit(solution)/shard_map/pallas_call | solution.py:242
  37.7 4.4 %collective-permute-done.9.other_ref = bf16[1,256,1024]{2,1,0:T(8,128)(2,1)S(1)} collective-permute-done((bf16[1,256,1024]{2,1,0:T(8,128)(2,1)S(1)}, bf16[1,256,1024]{2,1,0:T(8,128)(2,1)S(1)}, u32[]{:S(2)}, u32[]{:S(2)}) %collective-permute-start.9) | collective-permute-done | bytes 524320 | tf_op jit(solution)/shard_map/ppermute | solution.py:418
  42.1 2.8 %shard_map.88.refs_15_.refs_3_ = bf16[1024,256]{1,0:T(8,128)(2,1)S(1)} custom-call(s32[6]{0:T(128)S(1)} %stack.63.scalars, bf16[2,256,1024]{2,1,0:T(8,128)(2,1)S(1)} %copy-done.2, bf16[1,256,1024]{2,1,0:T(8,128)(2,1)S(1)} %collective-permute-done.9.other_ref, bf16[1024,2048]{1,0:T(8,128)(2,1)S(1)} %copy-done.4, bf16[1024,2048]{1,0:T(8,128)(2,1)S(1)} %copy-done.4), custom_call_target="tpu_custom_call" | custom-call | flops 21474836480 | bytes 125829120 | tf_op jit(solution)/shard_map/pallas_call | solution.py:242
  45.0 2.8 %collective-permute-done.2.refs_5_ = bf16[2,256,1024]{2,1,0:T(8,128)(2,1)} collective-permute-done((bf16[2,256,1024]{2,1,0:T(8,128)(2,1)}, bf16[2,256,1024]{2,1,0:T(8,128)(2,1)}, u32[]{:S(2)}, u32[]{:S(2)}) %collective-permute-start.2) | collective-permute-done | bytes 1048608 | tf_op jit(solution)/shard_map/ppermute | solution.py:423
  47.8 5.5 %shard_map.85 = (bf16[256,1024]{1,0:T(8,128)(2,1)S(1)}, bf16[2,256,1024]{2,1,0:T(8,128)(2,1)}, f32[2,256,1024]{2,1,0:T(8,128)S(1)}, bf16[2,256,2048]{2,1,0:T(8,1...) custom-call(s32[6]{0:T(128)S(1)} %stack.63.scalars, ...), custom_call_target="tpu_custom_call" | custom-call | flops 20132659200 | bytes 167772160 | tf_op jit(solution)/shard_map/pallas_call | solution.py:208
  53.3 5.5 %shard_map.86 = (bf16[256,1024]{1,0:T(8,128)(2,1)S(1)}, bf16[2,256,1024]{2,1,0:T(8,128)(2,1)}, f32[2,256,1024]{2,1,0:T(8,128)S(1)}, bf16[2,256,2048]{2,1,0:T(8,1...) custom-call(s32[6]{0:T(128)S(1)} %stack.63.scalars, ...), custom_call_target="tpu_custom_call", output_to_operand_aliasing={{0}: (11, {}), {1}: (12, {}), {2}: (13, {}), {3}: (14, {}),... | custom-call | flops 20132659200 | bytes 167772160 | tf_op jit(solution)/shard_map/pallas_call | solution.py:208
  60.8 2.9 %collective-permute-start.6 = (bf16[2,256,256]{2,1,0:T(8,128)(2,1)S(1)}, bf16[2,256,256]{2,1,0:T(8,128)(2,1)S(1)}, u32[]{:S(2)}, u32[]{:S(2)}) collective-permute-start(bf16[2,256,256]{2,1,0:T(8,128)(2,1)S(1)} %get-tuple-element.84), channel_id=1, source_target_pairs={{16,0},{18,2},{20,4},{22,6},{24,8},{26,10},{28,12},{30,14},{0,16},... | collective-permute-start | bytes 786440 | tf_op jit(solution)/shard_map/ppermute | solution.py:529
  63.8 4.5 %collective-permute-start.10 = (bf16[2,256,1024]{2,1,0:T(8,128)(2,1)S(1)}, bf16[2,256,1024]{2,1,0:T(8,128)(2,1)S(1)}, u32[]{:S(2)}, u32[]{:S(2)}) collective-permute-start(bf16[2,256,1024]{2,1,0:T(8,128)(2,1)S(1)} %pad_maximum_fusion.2), channel_id=1, source_target_pairs={{0,4},{2,6},{8,12},{10,14},{16,20},{18,22},{24,28},{26,30},{1,5},{... | collective-permute-start | bytes 3145736 | tf_op jit(solution)/shard_map/ppermute | solution.py:423
  68.5 5.6 %shard_map.87 = (bf16[256,1024]{1,0:T(8,128)(2,1)S(1)}, bf16[2,256,1024]{2,1,0:T(8,128)(2,1)}, f32[2,256,1024]{2,1,0:T(8,128)S(1)}, bf16[2,256,2048]{2,1,0:T(8,1...) custom-call(s32[6]{0:T(128)S(1)} %stack.63.scalars, ...), custom_call_target="tpu_custom_call", output_to_operand_aliasing={{0}: (11, {}), {1}: (12, {}), {2}: (13, {}), {3}: (14, {}),... | custom-call | flops 20132659200 | bytes 167772160 | tf_op jit(solution)/shard_map/pallas_call | solution.py:208
  75.0 2.9 %collective-permute-done.5.refs_6_.refs_7_ = bf16[2,256,256]{2,1,0:T(8,128)(2,1)S(1)} collective-permute-done((bf16[2,256,256]{2,1,0:T(8,128)(2,1)S(1)}, bf16[2,256,256]{2,1,0:T(8,128)(2,1)S(1)}, u32[]{:S(2)}, u32[]{:S(2)}) %collective-permute-start.5) | collective-permute-done | bytes 262176 | tf_op jit(solution)/shard_map/ppermute | solution.py:529
  78.0 5.4 %shard_map.89 = (bf16[256,1024]{1,0:T(8,128)(2,1)S(1)}, bf16[2,256,1024]{2,1,0:T(8,128)(2,1)}, f32[2,256,1024]{2,1,0:T(8,128)S(1)}, bf16[2,256,2048]{2,1,0:T(8,1...) custom-call(s32[6]{0:T(128)S(1)} %stack.63.scalars, ...), custom_call_target="tpu_custom_call", output_to_operand_aliasing={{0}: (11, {}), {1}: (12, {}), {2}: (13, {}), {3}: (14, {}),... | custom-call | flops 20132659200 | bytes 167772160 | tf_op jit(solution)/shard_map/pallas_call | solution.py:208
  85.1 3.1 %shard_map.90 = (bf16[256,1024]{1,0:T(8,128)(2,1)S(1)}, f32[256,1024]{1,0:T(8,128)S(1)}) custom-call(s32[6]{0:T(128)S(1)} %stack.63.scalars, bf16[256,1024]{1,0:T(8,128)(2,1)S(1)} %get-tuple-element.98.attn_ref, bf16[1024,2048]{1,0:T(8,128)(2,1)S(1)} %copy-done.4), custom_call_target="tpu_custom_call" | custom-call | flops 21474836480 | bytes 125829120 | tf_op jit(solution)/shard_map/pallas_call | solution.py:280
  90.5 5.3 %shard_map.91 = (bf16[256,1024]{1,0:T(8,128)(2,1)S(1)}, bf16[2,256,1024]{2,1,0:T(8,128)(2,1)}, f32[2,256,1024]{2,1,0:T(8,128)S(1)}, bf16[2,256,2048]{2,1,0:T(8,1...) custom-call(s32[6]{0:T(128)S(1)} %stack.63.scalars, ...), custom_call_target="tpu_custom_call", output_to_operand_aliasing={{1}: (11, {}), {3}: (12, {})} | custom-call | flops 20132659200 | bytes 167772160 | tf_op jit(solution)/shard_map/pallas_call | solution.py:208
  101.2 5.3 %shard_map.92 = (bf16[256,1024]{1,0:T(8,128)(2,1)S(1)}, bf16[2,256,1024]{2,1,0:T(8,128)(2,1)}, f32[2,256,1024]{2,1,0:T(8,128)S(1)}, bf16[2,256,2048]{2,1,0:T(8,1...) custom-call(s32[6]{0:T(128)S(1)} %stack.63.scalars, ...), custom_call_target="tpu_custom_call", output_to_operand_aliasing={{0}: (11, {}), {1}: (12, {}), {2}: (13, {}), {3}: (14, {}),... | custom-call | flops 20132659200 | bytes 167772160 | tf_op jit(solution)/shard_map/pallas_call | solution.py:208
  107.4 6.1 %collective-permute-done.19.refs_12_.refs_2_.refs_6_.refs_10_.refs_14_ = bf16[2,256,1024]{2,1,0:T(8,128)(2,1)S(1)} collective-permute-done((bf16[2,256,1024]{2,1,0:T(8,128)(2,1)S(1)}, bf16[2,256,1024]{2,1,0:T(8,128)(2,1)S(1)}, u32[]{:S(2)}, u32[]{:S(2)}) %collective-permute-start.19) | collective-permute-done | bytes 1048608 | tf_op jit(solution)/shard_map/ppermute | solution.py:482
  115.1 5.4 %shard_map.93 = (bf16[256,1024]{1,0:T(8,128)(2,1)S(1)}, bf16[2,256,1024]{2,1,0:T(8,128)(2,1)}, f32[2,256,1024]{2,1,0:T(8,128)S(1)}, bf16[2,256,2048]{2,1,0:T(8,1...) custom-call(s32[6]{0:T(128)S(1)} %stack.63.scalars, ...), custom_call_target="tpu_custom_call", output_to_operand_aliasing={{0}: (9, {}), {1}: (10, {}), {2}: (11, {}), {3}: (12, {})} | custom-call | flops 20132659200 | bytes 167772160 | tf_op jit(solution)/shard_map/pallas_call | solution.py:208
  124.6 5.4 %shard_map.94 = (bf16[256,1024]{1,0:T(8,128)(2,1)S(1)}, bf16[2,256,1024]{2,1,0:T(8,128)(2,1)}, f32[2,256,1024]{2,1,0:T(8,128)S(1)}, bf16[2,256,2048]{2,1,0:T(8,1...) custom-call(s32[6]{0:T(128)S(1)} %stack.63.scalars, ...), custom_call_target="tpu_custom_call", output_to_operand_aliasing={{0}: (9, {}), {1}: (10, {}), {2}: (11, {}), {3}: (12, {}), ... | custom-call | flops 20132659200 | bytes 167772160 | tf_op jit(solution)/shard_map/pallas_call | solution.py:208
  135.1 3.1 %shard_map.95 = (bf16[256,1024]{1,0:T(8,128)(2,1)S(1)}, f32[256,1024]{1,0:T(8,128)S(1)}) custom-call(s32[6]{0:T(128)S(1)} %stack.63.scalars, bf16[256,1024]{1,0:T(8,128)(2,1)S(1)} %get-tuple-element.129.attn_ref, bf16[1024,2048]{1,0:T(8,128)(2,1)S(1)} %copy-done.4), custom_call_target="tpu_custom_call" | custom-call | flops 21474836480 | bytes 125829120 | tf_op jit(solution)/shard_map/pallas_call | solution.py:280
  144.9 10.4 %collective-permute-done.25.refs_10_.refs_2_ = bf16[2,256,512]{2,1,0:T(8,128)(2,1)S(1)} collective-permute-done((bf16[2,256,512]{2,1,0:T(8,128)(2,1)S(1)}, bf16[2,256,512]{2,1,0:T(8,128)(2,1)S(1)}, u32[]{:S(2)}, u32[]{:S(2)}) %collective-permute-start.25) | collective-permute-done | bytes 524320 | tf_op jit(solution)/shard_map/ppermute | solution.py:482
  160.4 3.7 %collective-permute-done.23 = bf16[2,256,1024]{2,1,0:T(8,128)(2,1)S(1)} collective-permute-done((bf16[2,256,1024]{2,1,0:T(8,128)(2,1)S(1)}, bf16[2,256,1024]{2,1,0:T(8,128)(2,1)S(1)}, u32[]{:S(2)}, u32[]{:S(2)}) %collective-permute-start.23) | collective-permute-done | bytes 1048608 | tf_op jit(solution)/shard_map/ppermute | solution.py:418
  (77 shorter events, 52.4 us)
Async XLA Ops:
  3.5 41.4 %collective-permute-start.3 = (bf16[2,256,512]{2,1,0:T(8,128)(2,1)}, bf16[2,256,512]{2,1,0:T(8,128)(2,1)}, u32[]{:S(2)}, u32[]{:S(2)}) collective-permute-start(bf16[2,256,512]{2,1,0:T(8,128)(2,1)} %pad_maximum_fusion.4), channel_id=1, source_target_pairs={{0,8},{2,10},{4,12},{6,14},{16,24},{18,26},{20,28},{22,30},{1,9},{... | collective-permute-start | bytes 1572872 | tf_op jit(solution)/shard_map/ppermute | solution.py:438
  9.3 35.7 %collective-permute-start.4 = (bf16[2,256,512]{2,1,0:T(8,128)(2,1)}, bf16[2,256,512]{2,1,0:T(8,128)(2,1)}, u32[]{:S(2)}, u32[]{:S(2)}) collective-permute-start(bf16[2,256,512]{2,1,0:T(8,128)(2,1)} %pad_maximum_fusion.4), channel_id=1, source_target_pairs={{0,16},{2,18},{4,20},{6,22},{8,24},{10,26},{12,28},{14,30},{1,17},... | collective-permute-start | bytes 1572872 | tf_op jit(solution)/shard_map/ppermute | solution.py:438
  16.4 13.4 %collective-permute-start = (bf16[1,256,1024]{2,1,0:T(8,128)(2,1)}, bf16[1,256,1024]{2,1,0:T(8,128)(2,1)}, u32[]{:S(2)}, u32[]{:S(2)}) collective-permute-start(bf16[1,256,1024]{2,1,0:T(8,128)(2,1)} %slice.32), channel_id=1, source_target_pairs={{0,1},{1,0},{2,3},{3,2},{4,5},{5,4},{6,7},{7,6},{8,9},{9,8},{10,11... | collective-permute-start | bytes 1572872 | tf_op jit(solution)/shard_map/ppermute | solution.py:418
  20.0 27.8 %collective-permute-start.1 = (bf16[2,256,2048]{2,1,0:T(8,128)(2,1)}, bf16[2,256,2048]{2,1,0:T(8,128)(2,1)}, u32[]{:S(2)}, u32[]{:S(2)}) collective-permute-start(bf16[2,256,2048]{2,1,0:T(8,128)(2,1)} %pad_maximum_fusion), channel_id=1, source_target_pairs={{0,2},{4,6},{8,10},{12,14},{16,18},{20,22},{24,26},{28,30},{1,3},{... | collective-permute-start | bytes 6291464 | tf_op jit(solution)/shard_map/ppermute | solution.py:423
  23.8 24.0 %collective-permute-start.2 = (bf16[2,256,1024]{2,1,0:T(8,128)(2,1)}, bf16[2,256,1024]{2,1,0:T(8,128)(2,1)}, u32[]{:S(2)}, u32[]{:S(2)}) collective-permute-start(bf16[2,256,1024]{2,1,0:T(8,128)(2,1)} %pad_maximum_fusion.1), channel_id=1, source_target_pairs={{0,4},{2,6},{8,12},{10,14},{16,20},{18,22},{24,28},{26,30},{1,5},{... | collective-permute-start | bytes 3145736 | tf_op jit(solution)/shard_map/ppermute | solution.py:423
  29.9 12.2 %collective-permute-start.9 = (bf16[1,256,1024]{2,1,0:T(8,128)(2,1)S(1)}, bf16[1,256,1024]{2,1,0:T(8,128)(2,1)S(1)}, u32[]{:S(2)}, u32[]{:S(2)}) collective-permute-start(bf16[1,256,1024]{2,1,0:T(8,128)(2,1)S(1)} %slice.39), channel_id=1, source_target_pairs={{0,1},{1,0},{2,3},{3,2},{4,5},{5,4},{6,7},{7,6},{8,9},{9,8},{10,11... | collective-permute-start | bytes 1572872 | tf_op jit(solution)/shard_map/ppermute | solution.py:418
  53.3 15.2 %collective-permute-start.7 = (bf16[2,256,256]{2,1,0:T(8,128)(2,1)S(1)}, bf16[2,256,256]{2,1,0:T(8,128)(2,1)S(1)}, u32[]{:S(2)}, u32[]{:S(2)}) collective-permute-start(bf16[2,256,256]{2,1,0:T(8,128)(2,1)S(1)} %get-tuple-element.85), channel_id=1, source_target_pairs={{8,0},{10,2},{12,4},{14,6},{24,16},{26,18},{28,20},{30,22},{0,8},{... | collective-permute-start | bytes 786440 | tf_op jit(solution)/shard_map/ppermute | solution.py:529
  53.3 15.2 %collective-permute-start.8 = (bf16[2,256,256]{2,1,0:T(8,128)(2,1)S(1)}, bf16[2,256,256]{2,1,0:T(8,128)(2,1)S(1)}, u32[]{:S(2)}, u32[]{:S(2)}) collective-permute-start(bf16[2,256,256]{2,1,0:T(8,128)(2,1)S(1)} %get-tuple-element.86), channel_id=1, source_target_pairs={{16,0},{18,2},{20,4},{22,6},{24,8},{26,10},{28,12},{30,14},{0,16},... | collective-permute-start | bytes 786440 | tf_op jit(solution)/shard_map/ppermute | solution.py:529
  58.8 19.2 %collective-permute-start.5 = (bf16[2,256,256]{2,1,0:T(8,128)(2,1)S(1)}, bf16[2,256,256]{2,1,0:T(8,128)(2,1)S(1)}, u32[]{:S(2)}, u32[]{:S(2)}) collective-permute-start(bf16[2,256,256]{2,1,0:T(8,128)(2,1)S(1)} %get-tuple-element.83), channel_id=1, source_target_pairs={{8,0},{10,2},{12,4},{14,6},{24,16},{26,18},{28,20},{30,22},{0,8},{... | collective-permute-start | bytes 786440 | tf_op jit(solution)/shard_map/ppermute | solution.py:529
  60.8 17.2 %collective-permute-start.6 = (bf16[2,256,256]{2,1,0:T(8,128)(2,1)S(1)}, bf16[2,256,256]{2,1,0:T(8,128)(2,1)S(1)}, u32[]{:S(2)}, u32[]{:S(2)}) collective-permute-start(bf16[2,256,256]{2,1,0:T(8,128)(2,1)S(1)} %get-tuple-element.84), channel_id=1, source_target_pairs={{16,0},{18,2},{20,4},{22,6},{24,8},{26,10},{28,12},{30,14},{0,16},... | collective-permute-start | bytes 786440 | tf_op jit(solution)/shard_map/ppermute | solution.py:529
  63.8 26.6 %collective-permute-start.10 = (bf16[2,256,1024]{2,1,0:T(8,128)(2,1)S(1)}, bf16[2,256,1024]{2,1,0:T(8,128)(2,1)S(1)}, u32[]{:S(2)}, u32[]{:S(2)}) collective-permute-start(bf16[2,256,1024]{2,1,0:T(8,128)(2,1)S(1)} %pad_maximum_fusion.2), channel_id=1, source_target_pairs={{0,4},{2,6},{8,12},{10,14},{16,20},{18,22},{24,28},{26,30},{1,5},{... | collective-permute-start | bytes 3145736 | tf_op jit(solution)/shard_map/ppermute | solution.py:423
  74.1 15.1 %collective-permute-start.13 = (bf16[2,256,256]{2,1,0:T(8,128)(2,1)S(1)}, bf16[2,256,256]{2,1,0:T(8,128)(2,1)S(1)}, u32[]{:S(2)}, u32[]{:S(2)}) collective-permute-start(bf16[2,256,256]{2,1,0:T(8,128)(2,1)S(1)} %get-tuple-element.104), channel_id=1, source_target_pairs={{8,0},{10,2},{12,4},{14,6},{24,16},{26,18},{28,20},{30,22},{0,8},{... | collective-permute-start | bytes 786440 | tf_op jit(solution)/shard_map/ppermute | solution.py:529
  74.1 16.4 %collective-permute-start.14 = (bf16[2,256,256]{2,1,0:T(8,128)(2,1)S(1)}, bf16[2,256,256]{2,1,0:T(8,128)(2,1)S(1)}, u32[]{:S(2)}, u32[]{:S(2)}) collective-permute-start(bf16[2,256,256]{2,1,0:T(8,128)(2,1)S(1)} %get-tuple-element.105), channel_id=1, source_target_pairs={{16,0},{18,2},{20,4},{22,6},{24,8},{26,10},{28,12},{30,14},{0,16},... | collective-permute-start | bytes 786440 | tf_op jit(solution)/shard_map/ppermute | solution.py:529
  83.3 17.0 %collective-permute-start.11 = (bf16[2,256,256]{2,1,0:T(8,128)(2,1)S(1)}, bf16[2,256,256]{2,1,0:T(8,128)(2,1)S(1)}, u32[]{:S(2)}, u32[]{:S(2)}) collective-permute-start(bf16[2,256,256]{2,1,0:T(8,128)(2,1)S(1)} %get-tuple-element.102), channel_id=1, source_target_pairs={{8,0},{10,2},{12,4},{14,6},{24,16},{26,18},{28,20},{30,22},{0,8},{... | collective-permute-start | bytes 786440 | tf_op jit(solution)/shard_map/ppermute | solution.py:529
  83.3 17.9 %collective-permute-start.12 = (bf16[2,256,256]{2,1,0:T(8,128)(2,1)S(1)}, bf16[2,256,256]{2,1,0:T(8,128)(2,1)S(1)}, u32[]{:S(2)}, u32[]{:S(2)}) collective-permute-start(bf16[2,256,256]{2,1,0:T(8,128)(2,1)S(1)} %get-tuple-element.103), channel_id=1, source_target_pairs={{16,0},{18,2},{20,4},{22,6},{24,8},{26,10},{28,12},{30,14},{0,16},... | collective-permute-start | bytes 786440 | tf_op jit(solution)/shard_map/ppermute | solution.py:529
  89.1 24.4 %collective-permute-start.19 = (bf16[2,256,1024]{2,1,0:T(8,128)(2,1)S(1)}, bf16[2,256,1024]{2,1,0:T(8,128)(2,1)S(1)}, u32[]{:S(2)}, u32[]{:S(2)}) collective-permute-start(bf16[2,256,1024]{2,1,0:T(8,128)(2,1)S(1)} %get-tuple-element.121), channel_id=1, source_target_pairs={{4,0},{6,2},{12,8},{14,10},{20,16},{22,18},{28,24},{30,26},{5,1},{... | collective-permute-start | bytes 3145736 | tf_op jit(solution)/shard_map/ppermute | solution.py:482
  95.7 19.4 %collective-permute-start.17 = (bf16[2,256,256]{2,1,0:T(8,128)(2,1)S(1)}, bf16[2,256,256]{2,1,0:T(8,128)(2,1)S(1)}, u32[]{:S(2)}, u32[]{:S(2)}) collective-permute-start(bf16[2,256,256]{2,1,0:T(8,128)(2,1)S(1)} %get-tuple-element.115), channel_id=1, source_target_pairs={{8,0},{10,2},{12,4},{14,6},{24,16},{26,18},{28,20},{30,22},{0,8},{... | collective-permute-start | bytes 786440 | tf_op jit(solution)/shard_map/ppermute | solution.py:529
  96.8 18.3 %collective-permute-start.18 = (bf16[2,256,256]{2,1,0:T(8,128)(2,1)S(1)}, bf16[2,256,256]{2,1,0:T(8,128)(2,1)S(1)}, u32[]{:S(2)}, u32[]{:S(2)}) collective-permute-start(bf16[2,256,256]{2,1,0:T(8,128)(2,1)S(1)} %get-tuple-element.116), channel_id=1, source_target_pairs={{16,0},{18,2},{20,4},{22,6},{24,8},{26,10},{28,12},{30,14},{0,16},... | collective-permute-start | bytes 786440 | tf_op jit(solution)/shard_map/ppermute | solution.py:529
  106.5 16.6 %collective-permute-start.15 = (bf16[2,256,256]{2,1,0:T(8,128)(2,1)S(1)}, bf16[2,256,256]{2,1,0:T(8,128)(2,1)S(1)}, u32[]{:S(2)}, u32[]{:S(2)}) collective-permute-start(bf16[2,256,256]{2,1,0:T(8,128)(2,1)S(1)} %get-tuple-element.113), channel_id=1, source_target_pairs={{8,0},{10,2},{12,4},{14,6},{24,16},{26,18},{28,20},{30,22},{0,8},{... | collective-permute-start | bytes 786440 | tf_op jit(solution)/shard_map/ppermute | solution.py:529
  106.5 16.6 %collective-permute-start.16 = (bf16[2,256,256]{2,1,0:T(8,128)(2,1)S(1)}, bf16[2,256,256]{2,1,0:T(8,128)(2,1)S(1)}, u32[]{:S(2)}, u32[]{:S(2)}) collective-permute-start(bf16[2,256,256]{2,1,0:T(8,128)(2,1)S(1)} %get-tuple-element.114), channel_id=1, source_target_pairs={{16,0},{18,2},{20,4},{22,6},{24,8},{26,10},{28,12},{30,14},{0,16},... | collective-permute-start | bytes 786440 | tf_op jit(solution)/shard_map/ppermute | solution.py:529
  138.3 25.8 %collective-permute-start.23 = (bf16[2,256,1024]{2,1,0:T(8,128)(2,1)S(1)}, bf16[2,256,1024]{2,1,0:T(8,128)(2,1)S(1)}, u32[]{:S(2)}, u32[]{:S(2)}) collective-permute-start(bf16[2,256,1024]{2,1,0:T(8,128)(2,1)S(1)} %pad_maximum_fusion.3), channel_id=1, source_target_pairs={{0,1},{1,0},{2,3},{3,2},{4,5},{5,4},{6,7},{7,6},{8,9},{9,8},{10,11... | collective-permute-start | bytes 3145736 | tf_op jit(solution)/shard_map/ppermute | solution.py:418
  138.9 16.4 %collective-permute-start.25 = (bf16[2,256,512]{2,1,0:T(8,128)(2,1)S(1)}, bf16[2,256,512]{2,1,0:T(8,128)(2,1)S(1)}, u32[]{:S(2)}, u32[]{:S(2)}) collective-permute-start(bf16[2,256,512]{2,1,0:T(8,128)(2,1)S(1)} %get-tuple-element.140), channel_id=1, source_target_pairs={{4,0},{6,2},{12,8},{14,10},{20,16},{22,18},{28,24},{30,26},{5,1},{... | collective-permute-start | bytes 1572872 | tf_op jit(solution)/shard_map/ppermute | solution.py:482
  140.2 17.0 %collective-permute-start.26 = (bf16[2,256,256]{2,1,0:T(8,128)(2,1)S(1)}, bf16[2,256,256]{2,1,0:T(8,128)(2,1)S(1)}, u32[]{:S(2)}, u32[]{:S(2)}) collective-permute-start(bf16[2,256,256]{2,1,0:T(8,128)(2,1)S(1)} %get-tuple-element.141), channel_id=1, source_target_pairs={{8,0},{10,2},{12,4},{14,6},{24,16},{26,18},{28,20},{30,22},{9,1},{... | collective-permute-start | bytes 786440 | tf_op jit(solution)/shard_map/ppermute | solution.py:529
  141.5 17.6 %collective-permute-start.27 = (bf16[2,256,256]{2,1,0:T(8,128)(2,1)S(1)}, bf16[2,256,256]{2,1,0:T(8,128)(2,1)S(1)}, u32[]{:S(2)}, u32[]{:S(2)}) collective-permute-start(bf16[2,256,256]{2,1,0:T(8,128)(2,1)S(1)} %get-tuple-element.142), channel_id=1, source_target_pairs={{16,0},{18,2},{20,4},{22,6},{24,8},{26,10},{28,12},{30,14},{17,1},... | collective-permute-start | bytes 786440 | tf_op jit(solution)/shard_map/ppermute | solution.py:529
  (12 other events, 116.4 us)

commit v3 on v2

--- a/solution.py
+++ b/solution.py
@@ -487,7 +487,7 @@
         parts = [project(scalars, source, out_proj) for source in attn]
         sent = behind(jnp.stack([send for send, _ in parts]), *earlier)
         kept = jnp.stack([kept for _, kept in parts])
-        return kept, other_half(sent)
+        return kept, sent, other_half(sent)
 
     for t, chunk in enumerate(chunks):
         at = chunk[0]
@@ -540,8 +540,8 @@
             gates[7] = (back_coarse[1, 1],)
     last = arrived(count)
     send_down(1, 2, back_coarse[1, 1], *last)
-    kept, received = send_out(*last)
-    send_down(0, 0, *last)
+    kept, sent, received = send_out(*last)
+    send_down(0, 0, sent, *last)
     grads = finished(0, 4, grads)
     grads = finished(4, 7, grads)
     grads = finished(7, 8, grads)

time: 166 us -> 163 us (0.982)
  waiting for transfers between devices: 43.6 us -> 40.4 us
    ppermute x16, waiting for transfers between devices: 13.1 us -> 9.93 us  [body(): lax.ppermute(results[3 + len(coarse) + place_of], 'seq', pairs)]
  transfers between devices with their start and end apart: 28 -> 28, of which waited for: 15 -> 15; matrix products, arithmetic and copies ran while one was open for 3% -> 3% of each run, Pallas kernels for 34% -> 35%
where the time goes in v3:
time: 163 us; the launch traced here: 162 us
  Pallas kernels  61.6 us (38%)
  starting transfers between devices  47.6 us (29%)
  waiting for transfers between devices  40.4 us (25%)
  local copies, waits for them, and re-layouts  6.58 us (4%)
  other arithmetic  5.15 us (3%)
    pallas_call x8, Pallas kernels, chunk_call(): pl.pallas_call(partial(unit_kernel, levels, fine, coarse, has_next, len(a...  43.2 us
    ppermute x4, waiting for transfers between devices, send_down(): lax.ppermute(behind(down_buffers[level, index], *earlier), 'seq', down_pa...  18.1 us
    ppermute x16, starting transfers between devices, body(): lax.ppermute(results[3 + len(coarse) + place_of], 'seq', pairs)  16 us
    ppermute x3, starting transfers between devices, send_coarse(): lax.ppermute(packed(ups[level][index], *earlier), 'seq', up_pairs[level])  11.6 us
    ppermute x2, starting transfers between devices, body(): lax.ppermute(opening, 'seq', up_pairs[level])  11 us
    ppermute x16, waiting for transfers between devices, body(): lax.ppermute(results[3 + len(coarse) + place_of], 'seq', pairs)  9.93 us
    ppermute x3, waiting for transfers between devices, other_half(): return lax.ppermute(source, 'head', [(0, 1), (1, 0)])  9.54 us
    pallas_call x2, Pallas kernels, grad_project(): pl.pallas_call(grad_kernel, out_shape=jax.ShapeDtypeStruct((width, rows),...  6.9 us
  transfers between devices with their start and end apart: 28, of which 15 were waited for; matrix products, arithmetic and copies ran while one was open for 3% of the time, Pallas kernels for 35%

profile of v3, /device:TPU:0, one launch (start us, length us, event | category | flops | bytes accessed | tf_op | source)
XLA Modules:
  0.0 162.2 jit_solution(9174822050012453554)
XLA Ops:
  3.5 5.7 %collective-permute-start.3 = (bf16[2,256,512]{2,1,0:T(8,128)(2,1)}, bf16[2,256,512]{2,1,0:T(8,128)(2,1)}, u32[]{:S(2)}, u32[]{:S(2)}) collective-permute-start(bf16[2,256,512]{2,1,0:T(8,128)(2,1)} %pad_maximum_fusion.4), channel_id=1, source_target_pairs={{0,8},{2,10},{4,12},{6,14},{16,24},{18,26},{20,28},{22,30},{1,9},{... | collective-permute-start | bytes 1572872 | tf_op jit(solution)/shard_map/ppermute | solution.py:438
  9.3 5.3 %collective-permute-start.4 = (bf16[2,256,512]{2,1,0:T(8,128)(2,1)}, bf16[2,256,512]{2,1,0:T(8,128)(2,1)}, u32[]{:S(2)}, u32[]{:S(2)}) collective-permute-start(bf16[2,256,512]{2,1,0:T(8,128)(2,1)} %pad_maximum_fusion.4), channel_id=1, source_target_pairs={{0,16},{2,18},{4,20},{6,22},{8,24},{10,26},{12,28},{14,30},{1,17},... | collective-permute-start | bytes 1572872 | tf_op jit(solution)/shard_map/ppermute | solution.py:438
  20.0 2.7 %collective-permute-start.1 = (bf16[2,256,2048]{2,1,0:T(8,128)(2,1)}, bf16[2,256,2048]{2,1,0:T(8,128)(2,1)}, u32[]{:S(2)}, u32[]{:S(2)}) collective-permute-start(bf16[2,256,2048]{2,1,0:T(8,128)(2,1)} %pad_maximum_fusion), channel_id=1, source_target_pairs={{0,2},{4,6},{8,10},{12,14},{16,18},{20,22},{24,26},{28,30},{1,3},{... | collective-permute-start | bytes 6291464 | tf_op jit(solution)/shard_map/ppermute | solution.py:423
  23.8 4.4 %collective-permute-start.2 = (bf16[2,256,1024]{2,1,0:T(8,128)(2,1)}, bf16[2,256,1024]{2,1,0:T(8,128)(2,1)}, u32[]{:S(2)}, u32[]{:S(2)}) collective-permute-start(bf16[2,256,1024]{2,1,0:T(8,128)(2,1)} %pad_maximum_fusion.1), channel_id=1, source_target_pairs={{0,4},{2,6},{8,12},{10,14},{16,20},{18,22},{24,28},{26,30},{1,5},{... | collective-permute-start | bytes 3145736 | tf_op jit(solution)/shard_map/ppermute | solution.py:423
  33.6 4.1 %shard_map.84.refs_3_ = bf16[1024,256]{1,0:T(8,128)(2,1)S(1)} custom-call(s32[6]{0:T(128)S(1)} %stack.63.scalars, bf16[2,256,1024]{2,1,0:T(8,128)(2,1)S(1)} %copy-done.2, bf16[1,256,1024]{2,1,0:T(8,128)(2,1)} %collective-permute-done.other_ref, bf16[1024,2048]{1,0:T(8,128)(2,1)S(1)} %copy-done.3, bf16[1024,2048]{1,0:T(8,128)(2,1)S(1)} %copy-done.3), custom_call_target="tpu_custom_call" | custom-call | flops 21474836480 | bytes 125829120 | tf_op jit(solution)/shard_map/pallas_call | solution.py:242
  37.7 4.4 %collective-permute-done.9.other_ref = bf16[1,256,1024]{2,1,0:T(8,128)(2,1)S(1)} collective-permute-done((bf16[1,256,1024]{2,1,0:T(8,128)(2,1)S(1)}, bf16[1,256,1024]{2,1,0:T(8,128)(2,1)S(1)}, u32[]{:S(2)}, u32[]{:S(2)}) %collective-permute-start.9) | collective-permute-done | bytes 524320 | tf_op jit(solution)/shard_map/ppermute | solution.py:418
  42.1 2.8 %shard_map.88.refs_15_.refs_3_ = bf16[1024,256]{1,0:T(8,128)(2,1)S(1)} custom-call(s32[6]{0:T(128)S(1)} %stack.63.scalars, bf16[2,256,1024]{2,1,0:T(8,128)(2,1)S(1)} %copy-done.2, bf16[1,256,1024]{2,1,0:T(8,128)(2,1)S(1)} %collective-permute-done.9.other_ref, bf16[1024,2048]{1,0:T(8,128)(2,1)S(1)} %copy-done.4, bf16[1024,2048]{1,0:T(8,128)(2,1)S(1)} %copy-done.4), custom_call_target="tpu_custom_call" | custom-call | flops 21474836480 | bytes 125829120 | tf_op jit(solution)/shard_map/pallas_call | solution.py:242
  45.0 2.8 %collective-permute-done.2.refs_5_ = bf16[2,256,1024]{2,1,0:T(8,128)(2,1)} collective-permute-done((bf16[2,256,1024]{2,1,0:T(8,128)(2,1)}, bf16[2,256,1024]{2,1,0:T(8,128)(2,1)}, u32[]{:S(2)}, u32[]{:S(2)}) %collective-permute-start.2) | collective-permute-done | bytes 1048608 | tf_op jit(solution)/shard_map/ppermute | solution.py:423
  47.8 5.5 %shard_map.85 = (bf16[256,1024]{1,0:T(8,128)(2,1)S(1)}, bf16[2,256,1024]{2,1,0:T(8,128)(2,1)}, f32[2,256,1024]{2,1,0:T(8,128)S(1)}, bf16[2,256,2048]{2,1,0:T(8,1...) custom-call(s32[6]{0:T(128)S(1)} %stack.63.scalars, ...), custom_call_target="tpu_custom_call" | custom-call | flops 20132659200 | bytes 167772160 | tf_op jit(solution)/shard_map/pallas_call | solution.py:208
  53.3 5.5 %shard_map.86 = (bf16[256,1024]{1,0:T(8,128)(2,1)S(1)}, bf16[2,256,1024]{2,1,0:T(8,128)(2,1)}, f32[2,256,1024]{2,1,0:T(8,128)S(1)}, bf16[2,256,2048]{2,1,0:T(8,1...) custom-call(s32[6]{0:T(128)S(1)} %stack.63.scalars, ...), custom_call_target="tpu_custom_call", output_to_operand_aliasing={{0}: (11, {}), {1}: (12, {}), {2}: (13, {}), {3}: (14, {}),... | custom-call | flops 20132659200 | bytes 167772160 | tf_op jit(solution)/shard_map/pallas_call | solution.py:208
  60.8 2.9 %collective-permute-start.6 = (bf16[2,256,256]{2,1,0:T(8,128)(2,1)S(1)}, bf16[2,256,256]{2,1,0:T(8,128)(2,1)S(1)}, u32[]{:S(2)}, u32[]{:S(2)}) collective-permute-start(bf16[2,256,256]{2,1,0:T(8,128)(2,1)S(1)} %get-tuple-element.84), channel_id=1, source_target_pairs={{16,0},{18,2},{20,4},{22,6},{24,8},{26,10},{28,12},{30,14},{0,16},... | collective-permute-start | bytes 786440 | tf_op jit(solution)/shard_map/ppermute | solution.py:529
  63.8 4.5 %collective-permute-start.10 = (bf16[2,256,1024]{2,1,0:T(8,128)(2,1)S(1)}, bf16[2,256,1024]{2,1,0:T(8,128)(2,1)S(1)}, u32[]{:S(2)}, u32[]{:S(2)}) collective-permute-start(bf16[2,256,1024]{2,1,0:T(8,128)(2,1)S(1)} %pad_maximum_fusion.2), channel_id=1, source_target_pairs={{0,4},{2,6},{8,12},{10,14},{16,20},{18,22},{24,28},{26,30},{1,5},{... | collective-permute-start | bytes 3145736 | tf_op jit(solution)/shard_map/ppermute | solution.py:423
  68.5 5.6 %shard_map.87 = (bf16[256,1024]{1,0:T(8,128)(2,1)S(1)}, bf16[2,256,1024]{2,1,0:T(8,128)(2,1)}, f32[2,256,1024]{2,1,0:T(8,128)S(1)}, bf16[2,256,2048]{2,1,0:T(8,1...) custom-call(s32[6]{0:T(128)S(1)} %stack.63.scalars, ...), custom_call_target="tpu_custom_call", output_to_operand_aliasing={{0}: (11, {}), {1}: (12, {}), {2}: (13, {}), {3}: (14, {}),... | custom-call | flops 20132659200 | bytes 167772160 | tf_op jit(solution)/shard_map/pallas_call | solution.py:208
  75.0 2.9 %collective-permute-done.5.refs_6_.refs_7_ = bf16[2,256,256]{2,1,0:T(8,128)(2,1)S(1)} collective-permute-done((bf16[2,256,256]{2,1,0:T(8,128)(2,1)S(1)}, bf16[2,256,256]{2,1,0:T(8,128)(2,1)S(1)}, u32[]{:S(2)}, u32[]{:S(2)}) %collective-permute-start.5) | collective-permute-done | bytes 262176 | tf_op jit(solution)/shard_map/ppermute | solution.py:529
  78.0 5.4 %shard_map.89 = (bf16[256,1024]{1,0:T(8,128)(2,1)S(1)}, bf16[2,256,1024]{2,1,0:T(8,128)(2,1)}, f32[2,256,1024]{2,1,0:T(8,128)S(1)}, bf16[2,256,2048]{2,1,0:T(8,1...) custom-call(s32[6]{0:T(128)S(1)} %stack.63.scalars, ...), custom_call_target="tpu_custom_call", output_to_operand_aliasing={{0}: (11, {}), {1}: (12, {}), {2}: (13, {}), {3}: (14, {}),... | custom-call | flops 20132659200 | bytes 167772160 | tf_op jit(solution)/shard_map/pallas_call | solution.py:208
  85.1 3.1 %shard_map.90 = (bf16[256,1024]{1,0:T(8,128)(2,1)S(1)}, f32[256,1024]{1,0:T(8,128)S(1)}) custom-call(s32[6]{0:T(128)S(1)} %stack.63.scalars, bf16[256,1024]{1,0:T(8,128)(2,1)S(1)} %get-tuple-element.98.attn_ref, bf16[1024,2048]{1,0:T(8,128)(2,1)S(1)} %copy-done.4), custom_call_target="tpu_custom_call" | custom-call | flops 21474836480 | bytes 125829120 | tf_op jit(solution)/shard_map/pallas_call | solution.py:280
  90.5 5.3 %shard_map.91 = (bf16[256,1024]{1,0:T(8,128)(2,1)S(1)}, bf16[2,256,1024]{2,1,0:T(8,128)(2,1)}, f32[2,256,1024]{2,1,0:T(8,128)S(1)}, bf16[2,256,2048]{2,1,0:T(8,1...) custom-call(s32[6]{0:T(128)S(1)} %stack.63.scalars, ...), custom_call_target="tpu_custom_call", output_to_operand_aliasing={{1}: (11, {}), {3}: (12, {})} | custom-call | flops 20132659200 | bytes 167772160 | tf_op jit(solution)/shard_map/pallas_call | solution.py:208
  101.2 5.3 %shard_map.92 = (bf16[256,1024]{1,0:T(8,128)(2,1)S(1)}, bf16[2,256,1024]{2,1,0:T(8,128)(2,1)}, f32[2,256,1024]{2,1,0:T(8,128)S(1)}, bf16[2,256,2048]{2,1,0:T(8,1...) custom-call(s32[6]{0:T(128)S(1)} %stack.63.scalars, ...), custom_call_target="tpu_custom_call", output_to_operand_aliasing={{0}: (11, {}), {1}: (12, {}), {2}: (13, {}), {3}: (14, {}),... | custom-call | flops 20132659200 | bytes 167772160 | tf_op jit(solution)/shard_map/pallas_call | solution.py:208
  107.4 6.1 %collective-permute-done.19.refs_12_.refs_2_.refs_6_.refs_10_.refs_14_ = bf16[2,256,1024]{2,1,0:T(8,128)(2,1)S(1)} collective-permute-done((bf16[2,256,1024]{2,1,0:T(8,128)(2,1)S(1)}, bf16[2,256,1024]{2,1,0:T(8,128)(2,1)S(1)}, u32[]{:S(2)}, u32[]{:S(2)}) %collective-permute-start.19) | collective-permute-done | bytes 1048608 | tf_op jit(solution)/shard_map/ppermute | solution.py:482
  115.1 5.4 %shard_map.93 = (bf16[256,1024]{1,0:T(8,128)(2,1)S(1)}, bf16[2,256,1024]{2,1,0:T(8,128)(2,1)}, f32[2,256,1024]{2,1,0:T(8,128)S(1)}, bf16[2,256,2048]{2,1,0:T(8,1...) custom-call(s32[6]{0:T(128)S(1)} %stack.63.scalars, ...), custom_call_target="tpu_custom_call", output_to_operand_aliasing={{0}: (9, {}), {1}: (10, {}), {2}: (11, {}), {3}: (12, {})} | custom-call | flops 20132659200 | bytes 167772160 | tf_op jit(solution)/shard_map/pallas_call | solution.py:208
  124.6 5.4 %shard_map.94 = (bf16[256,1024]{1,0:T(8,128)(2,1)S(1)}, bf16[2,256,1024]{2,1,0:T(8,128)(2,1)}, f32[2,256,1024]{2,1,0:T(8,128)S(1)}, bf16[2,256,2048]{2,1,0:T(8,1...) custom-call(s32[6]{0:T(128)S(1)} %stack.63.scalars, ...), custom_call_target="tpu_custom_call", output_to_operand_aliasing={{0}: (9, {}), {1}: (10, {}), {2}: (11, {}), {3}: (12, {}), ... | custom-call | flops 20132659200 | bytes 167772160 | tf_op jit(solution)/shard_map/pallas_call | solution.py:208
  130.0 3.0 %shard_map.95 = (bf16[256,1024]{1,0:T(8,128)(2,1)S(1)}, f32[256,1024]{1,0:T(8,128)S(1)}) custom-call(s32[6]{0:T(128)S(1)} %stack.63.scalars, bf16[256,1024]{1,0:T(8,128)(2,1)S(1)} %get-tuple-element.129.attn_ref, bf16[1024,2048]{1,0:T(8,128)(2,1)S(1)} %copy-done.4), custom_call_target="tpu_custom_call" | custom-call | flops 21474836480 | bytes 125829120 | tf_op jit(solution)/shard_map/pallas_call | solution.py:280
  142.0 10.1 %collective-permute-done.25.refs_10_.refs_2_ = bf16[2,256,512]{2,1,0:T(8,128)(2,1)S(1)} collective-permute-done((bf16[2,256,512]{2,1,0:T(8,128)(2,1)S(1)}, bf16[2,256,512]{2,1,0:T(8,128)(2,1)S(1)}, u32[]{:S(2)}, u32[]{:S(2)}) %collective-permute-start.25) | collective-permute-done | bytes 524320 | tf_op jit(solution)/shard_map/ppermute | solution.py:482
  157.2 3.7 %collective-permute-done.23 = bf16[2,256,1024]{2,1,0:T(8,128)(2,1)S(1)} collective-permute-done((bf16[2,256,1024]{2,1,0:T(8,128)(2,1)S(1)}, bf16[2,256,1024]{2,1,0:T(8,128)(2,1)S(1)}, u32[]{:S(2)}, u32[]{:S(2)}) %collective-permute-start.23) | collective-permute-done | bytes 1048608 | tf_op jit(solution)/shard_map/ppermute | solution.py:418
  (77 shorter events, 49.5 us)
Async XLA Ops:
  3.5 41.4 %collective-permute-start.3 = (bf16[2,256,512]{2,1,0:T(8,128)(2,1)}, bf16[2,256,512]{2,1,0:T(8,128)(2,1)}, u32[]{:S(2)}, u32[]{:S(2)}) collective-permute-start(bf16[2,256,512]{2,1,0:T(8,128)(2,1)} %pad_maximum_fusion.4), channel_id=1, source_target_pairs={{0,8},{2,10},{4,12},{6,14},{16,24},{18,26},{20,28},{22,30},{1,9},{... | collective-permute-start | bytes 1572872 | tf_op jit(solution)/shard_map/ppermute | solution.py:438
  9.3 35.7 %collective-permute-start.4 = (bf16[2,256,512]{2,1,0:T(8,128)(2,1)}, bf16[2,256,512]{2,1,0:T(8,128)(2,1)}, u32[]{:S(2)}, u32[]{:S(2)}) collective-permute-start(bf16[2,256,512]{2,1,0:T(8,128)(2,1)} %pad_maximum_fusion.4), channel_id=1, source_target_pairs={{0,16},{2,18},{4,20},{6,22},{8,24},{10,26},{12,28},{14,30},{1,17},... | collective-permute-start | bytes 1572872 | tf_op jit(solution)/shard_map/ppermute | solution.py:438
  16.4 13.4 %collective-permute-start = (bf16[1,256,1024]{2,1,0:T(8,128)(2,1)}, bf16[1,256,1024]{2,1,0:T(8,128)(2,1)}, u32[]{:S(2)}, u32[]{:S(2)}) collective-permute-start(bf16[1,256,1024]{2,1,0:T(8,128)(2,1)} %slice.32), channel_id=1, source_target_pairs={{0,1},{1,0},{2,3},{3,2},{4,5},{5,4},{6,7},{7,6},{8,9},{9,8},{10,11... | collective-permute-start | bytes 1572872 | tf_op jit(solution)/shard_map/ppermute | solution.py:418
  20.0 27.8 %collective-permute-start.1 = (bf16[2,256,2048]{2,1,0:T(8,128)(2,1)}, bf16[2,256,2048]{2,1,0:T(8,128)(2,1)}, u32[]{:S(2)}, u32[]{:S(2)}) collective-permute-start(bf16[2,256,2048]{2,1,0:T(8,128)(2,1)} %pad_maximum_fusion), channel_id=1, source_target_pairs={{0,2},{4,6},{8,10},{12,14},{16,18},{20,22},{24,26},{28,30},{1,3},{... | collective-permute-start | bytes 6291464 | tf_op jit(solution)/shard_map/ppermute | solution.py:423
  23.8 24.0 %collective-permute-start.2 = (bf16[2,256,1024]{2,1,0:T(8,128)(2,1)}, bf16[2,256,1024]{2,1,0:T(8,128)(2,1)}, u32[]{:S(2)}, u32[]{:S(2)}) collective-permute-start(bf16[2,256,1024]{2,1,0:T(8,128)(2,1)} %pad_maximum_fusion.1), channel_id=1, source_target_pairs={{0,4},{2,6},{8,12},{10,14},{16,20},{18,22},{24,28},{26,30},{1,5},{... | collective-permute-start | bytes 3145736 | tf_op jit(solution)/shard_map/ppermute | solution.py:423
  53.3 15.2 %collective-permute-start.7 = (bf16[2,256,256]{2,1,0:T(8,128)(2,1)S(1)}, bf16[2,256,256]{2,1,0:T(8,128)(2,1)S(1)}, u32[]{:S(2)}, u32[]{:S(2)}) collective-permute-start(bf16[2,256,256]{2,1,0:T(8,128)(2,1)S(1)} %get-tuple-element.85), channel_id=1, source_target_pairs={{8,0},{10,2},{12,4},{14,6},{24,16},{26,18},{28,20},{30,22},{0,8},{... | collective-permute-start | bytes 786440 | tf_op jit(solution)/shard_map/ppermute | solution.py:529
  53.3 15.2 %collective-permute-start.8 = (bf16[2,256,256]{2,1,0:T(8,128)(2,1)S(1)}, bf16[2,256,256]{2,1,0:T(8,128)(2,1)S(1)}, u32[]{:S(2)}, u32[]{:S(2)}) collective-permute-start(bf16[2,256,256]{2,1,0:T(8,128)(2,1)S(1)} %get-tuple-element.86), channel_id=1, source_target_pairs={{16,0},{18,2},{20,4},{22,6},{24,8},{26,10},{28,12},{30,14},{0,16},... | collective-permute-start | bytes 786440 | tf_op jit(solution)/shard_map/ppermute | solution.py:529
  58.8 19.2 %collective-permute-start.5 = (bf16[2,256,256]{2,1,0:T(8,128)(2,1)S(1)}, bf16[2,256,256]{2,1,0:T(8,128)(2,1)S(1)}, u32[]{:S(2)}, u32[]{:S(2)}) collective-permute-start(bf16[2,256,256]{2,1,0:T(8,128)(2,1)S(1)} %get-tuple-element.83), channel_id=1, source_target_pairs={{8,0},{10,2},{12,4},{14,6},{24,16},{26,18},{28,20},{30,22},{0,8},{... | collective-permute-start | bytes 786440 | tf_op jit(solution)/shard_map/ppermute | solution.py:529
  60.8 17.2 %collective-permute-start.6 = (bf16[2,256,256]{2,1,0:T(8,128)(2,1)S(1)}, bf16[2,256,256]{2,1,0:T(8,128)(2,1)S(1)}, u32[]{:S(2)}, u32[]{:S(2)}) collective-permute-start(bf16[2,256,256]{2,1,0:T(8,128)(2,1)S(1)} %get-tuple-element.84), channel_id=1, source_target_pairs={{16,0},{18,2},{20,4},{22,6},{24,8},{26,10},{28,12},{30,14},{0,16},... | collective-permute-start | bytes 786440 | tf_op jit(solution)/shard_map/ppermute | solution.py:529
  63.8 26.6 %collective-permute-start.10 = (bf16[2,256,1024]{2,1,0:T(8,128)(2,1)S(1)}, bf16[2,256,1024]{2,1,0:T(8,128)(2,1)S(1)}, u32[]{:S(2)}, u32[]{:S(2)}) collective-permute-start(bf16[2,256,1024]{2,1,0:T(8,128)(2,1)S(1)} %pad_maximum_fusion.2), channel_id=1, source_target_pairs={{0,4},{2,6},{8,12},{10,14},{16,20},{18,22},{24,28},{26,30},{1,5},{... | collective-permute-start | bytes 3145736 | tf_op jit(solution)/shard_map/ppermute | solution.py:423
  74.1 15.1 %collective-permute-start.13 = (bf16[2,256,256]{2,1,0:T(8,128)(2,1)S(1)}, bf16[2,256,256]{2,1,0:T(8,128)(2,1)S(1)}, u32[]{:S(2)}, u32[]{:S(2)}) collective-permute-start(bf16[2,256,256]{2,1,0:T(8,128)(2,1)S(1)} %get-tuple-element.104), channel_id=1, source_target_pairs={{8,0},{10,2},{12,4},{14,6},{24,16},{26,18},{28,20},{30,22},{0,8},{... | collective-permute-start | bytes 786440 | tf_op jit(solution)/shard_map/ppermute | solution.py:529
  74.1 16.4 %collective-permute-start.14 = (bf16[2,256,256]{2,1,0:T(8,128)(2,1)S(1)}, bf16[2,256,256]{2,1,0:T(8,128)(2,1)S(1)}, u32[]{:S(2)}, u32[]{:S(2)}) collective-permute-start(bf16[2,256,256]{2,1,0:T(8,128)(2,1)S(1)} %get-tuple-element.105), channel_id=1, source_target_pairs={{16,0},{18,2},{20,4},{22,6},{24,8},{26,10},{28,12},{30,14},{0,16},... | collective-permute-start | bytes 786440 | tf_op jit(solution)/shard_map/ppermute | solution.py:529
  83.3 17.0 %collective-permute-start.11 = (bf16[2,256,256]{2,1,0:T(8,128)(2,1)S(1)}, bf16[2,256,256]{2,1,0:T(8,128)(2,1)S(1)}, u32[]{:S(2)}, u32[]{:S(2)}) collective-permute-start(bf16[2,256,256]{2,1,0:T(8,128)(2,1)S(1)} %get-tuple-element.102), channel_id=1, source_target_pairs={{8,0},{10,2},{12,4},{14,6},{24,16},{26,18},{28,20},{30,22},{0,8},{... | collective-permute-start | bytes 786440 | tf_op jit(solution)/shard_map/ppermute | solution.py:529
  83.3 17.9 %collective-permute-start.12 = (bf16[2,256,256]{2,1,0:T(8,128)(2,1)S(1)}, bf16[2,256,256]{2,1,0:T(8,128)(2,1)S(1)}, u32[]{:S(2)}, u32[]{:S(2)}) collective-permute-start(bf16[2,256,256]{2,1,0:T(8,128)(2,1)S(1)} %get-tuple-element.103), channel_id=1, source_target_pairs={{16,0},{18,2},{20,4},{22,6},{24,8},{26,10},{28,12},{30,14},{0,16},... | collective-permute-start | bytes 786440 | tf_op jit(solution)/shard_map/ppermute | solution.py:529
  89.1 24.4 %collective-permute-start.19 = (bf16[2,256,1024]{2,1,0:T(8,128)(2,1)S(1)}, bf16[2,256,1024]{2,1,0:T(8,128)(2,1)S(1)}, u32[]{:S(2)}, u32[]{:S(2)}) collective-permute-start(bf16[2,256,1024]{2,1,0:T(8,128)(2,1)S(1)} %get-tuple-element.121), channel_id=1, source_target_pairs={{4,0},{6,2},{12,8},{14,10},{20,16},{22,18},{28,24},{30,26},{5,1},{... | collective-permute-start | bytes 3145736 | tf_op jit(solution)/shard_map/ppermute | solution.py:482
  95.7 19.4 %collective-permute-start.17 = (bf16[2,256,256]{2,1,0:T(8,128)(2,1)S(1)}, bf16[2,256,256]{2,1,0:T(8,128)(2,1)S(1)}, u32[]{:S(2)}, u32[]{:S(2)}) collective-permute-start(bf16[2,256,256]{2,1,0:T(8,128)(2,1)S(1)} %get-tuple-element.115), channel_id=1, source_target_pairs={{8,0},{10,2},{12,4},{14,6},{24,16},{26,18},{28,20},{30,22},{0,8},{... | collective-permute-start | bytes 786440 | tf_op jit(solution)/shard_map/ppermute | solution.py:529
  96.8 18.3 %collective-permute-start.18 = (bf16[2,256,256]{2,1,0:T(8,128)(2,1)S(1)}, bf16[2,256,256]{2,1,0:T(8,128)(2,1)S(1)}, u32[]{:S(2)}, u32[]{:S(2)}) collective-permute-start(bf16[2,256,256]{2,1,0:T(8,128)(2,1)S(1)} %get-tuple-element.116), channel_id=1, source_target_pairs={{16,0},{18,2},{20,4},{22,6},{24,8},{26,10},{28,12},{30,14},{0,16},... | collective-permute-start | bytes 786440 | tf_op jit(solution)/shard_map/ppermute | solution.py:529
  106.5 16.6 %collective-permute-start.15 = (bf16[2,256,256]{2,1,0:T(8,128)(2,1)S(1)}, bf16[2,256,256]{2,1,0:T(8,128)(2,1)S(1)}, u32[]{:S(2)}, u32[]{:S(2)}) collective-permute-start(bf16[2,256,256]{2,1,0:T(8,128)(2,1)S(1)} %get-tuple-element.113), channel_id=1, source_target_pairs={{8,0},{10,2},{12,4},{14,6},{24,16},{26,18},{28,20},{30,22},{0,8},{... | collective-permute-start | bytes 786440 | tf_op jit(solution)/shard_map/ppermute | solution.py:529
  106.5 16.6 %collective-permute-start.16 = (bf16[2,256,256]{2,1,0:T(8,128)(2,1)S(1)}, bf16[2,256,256]{2,1,0:T(8,128)(2,1)S(1)}, u32[]{:S(2)}, u32[]{:S(2)}) collective-permute-start(bf16[2,256,256]{2,1,0:T(8,128)(2,1)S(1)} %get-tuple-element.114), channel_id=1, source_target_pairs={{16,0},{18,2},{20,4},{22,6},{24,8},{26,10},{28,12},{30,14},{0,16},... | collective-permute-start | bytes 786440 | tf_op jit(solution)/shard_map/ppermute | solution.py:529
  120.5 12.7 %collective-permute-start.21 = (bf16[2,256,256]{2,1,0:T(8,128)(2,1)S(1)}, bf16[2,256,256]{2,1,0:T(8,128)(2,1)S(1)}, u32[]{:S(2)}, u32[]{:S(2)}) collective-permute-start(bf16[2,256,256]{2,1,0:T(8,128)(2,1)S(1)} %get-tuple-element.133), channel_id=1, source_target_pairs={{8,0},{10,2},{12,4},{14,6},{24,16},{26,18},{28,20},{30,22},{9,1},{... | collective-permute-start | bytes 786440 | tf_op jit(solution)/shard_map/ppermute | solution.py:529
  135.1 25.8 %collective-permute-start.23 = (bf16[2,256,1024]{2,1,0:T(8,128)(2,1)S(1)}, bf16[2,256,1024]{2,1,0:T(8,128)(2,1)S(1)}, u32[]{:S(2)}, u32[]{:S(2)}) collective-permute-start(bf16[2,256,1024]{2,1,0:T(8,128)(2,1)S(1)} %pad_maximum_fusion.3), channel_id=1, source_target_pairs={{0,1},{1,0},{2,3},{3,2},{4,5},{5,4},{6,7},{7,6},{8,9},{9,8},{10,11... | collective-permute-start | bytes 3145736 | tf_op jit(solution)/shard_map/ppermute | solution.py:418
  135.7 16.4 %collective-permute-start.25 = (bf16[2,256,512]{2,1,0:T(8,128)(2,1)S(1)}, bf16[2,256,512]{2,1,0:T(8,128)(2,1)S(1)}, u32[]{:S(2)}, u32[]{:S(2)}) collective-permute-start(bf16[2,256,512]{2,1,0:T(8,128)(2,1)S(1)} %get-tuple-element.140), channel_id=1, source_target_pairs={{4,0},{6,2},{12,8},{14,10},{20,16},{22,18},{28,24},{30,26},{5,1},{... | collective-permute-start | bytes 1572872 | tf_op jit(solution)/shard_map/ppermute | solution.py:482
  137.0 17.0 %collective-permute-start.26 = (bf16[2,256,256]{2,1,0:T(8,128)(2,1)S(1)}, bf16[2,256,256]{2,1,0:T(8,128)(2,1)S(1)}, u32[]{:S(2)}, u32[]{:S(2)}) collective-permute-start(bf16[2,256,256]{2,1,0:T(8,128)(2,1)S(1)} %get-tuple-element.141), channel_id=1, source_target_pairs={{8,0},{10,2},{12,4},{14,6},{24,16},{26,18},{28,20},{30,22},{9,1},{... | collective-permute-start | bytes 786440 | tf_op jit(solution)/shard_map/ppermute | solution.py:529
  138.3 17.6 %collective-permute-start.27 = (bf16[2,256,256]{2,1,0:T(8,128)(2,1)S(1)}, bf16[2,256,256]{2,1,0:T(8,128)(2,1)S(1)}, u32[]{:S(2)}, u32[]{:S(2)}) collective-permute-start(bf16[2,256,256]{2,1,0:T(8,128)(2,1)S(1)} %get-tuple-element.142), channel_id=1, source_target_pairs={{16,0},{18,2},{20,4},{22,6},{24,8},{26,10},{28,12},{30,14},{17,1},... | collective-permute-start | bytes 786440 | tf_op jit(solution)/shard_map/ppermute | solution.py:529
  (12 other events, 114.5 us)
